TPU v7x, 256 devices: a whole 4x4x8 slice. The times are simulated.
256 devices in a mesh: tile: 64 (over x, z, core), pair: 4 (over y).
Axes of the slice: x: 4, y: 4, z: 8, core: 2. Of those that a mesh axis runs over, the one named last changes fastest.
Arguments:
- amplitudes: bfloat16 [64, 3072, 1024], P('tile', 'pair'), may hold values from -6 to 6
- integrals: bfloat16 [64, 4, 1024, 1024], P('tile', None, 'pair'), may hold values from -0.09375 to 0.09375
- residual_in: float32 [64, 3072, 1024], P('tile', 'pair'), may hold values from -6 to 6
- shape_cols: int32 [64, 4], P('tile'), may hold values from -1 to 63, as said below
Outputs:
- residual_out: float32 [64, 3072, 1024], P('tile', 'pair')
Inputs may be any that keep to these rules, and one draw needn't show every extreme that they name: `shape_cols`: row p lists p itself first, then 4 - 1 distinct tile pairs p + o with 0 < |o| <= 2, where a tile pair outside 0 to 63 is written -1.
All inputs are finite; a program needn't handle non-finite values.
Results may differ from a plain program's by a relative error of at most 0.0003.
Values may be sent and summed in bfloat16 or wider, within the bound.
No kernel may reach another device: no remote copies, remote signals or barrier semaphores. Data moves between devices by JAX's collectives and lax.ppermute only.
A program may use at most 128 MiB of HBM per device.

v0:
```python
import jax
import jax.numpy as jnp
from jax import lax
from jax.sharding import PartitionSpec as P

REACH = 2


def shifted(block, axis, distance):
    devices = range(lax.axis_size(axis))
    route = [(i - distance, i) for i in devices if i - distance in devices]
    return lax.ppermute(block, axis, route)


def shards(amplitudes, integrals, residual_in, shape_cols):
    myself = lax.axis_index("tile")
    own_tile = amplitudes[0]
    lower = []
    current = own_tile
    for step in range(REACH):
        current = shifted(current, "tile", 1)
        lower.append(current)
    higher = []
    current = own_tile
    for step in range(REACH):
        current = shifted(current, "tile", -1)
        higher.append(current)
    ordered = lower[::-1] + [own_tile] + higher
    window = jnp.stack(ordered, axis=0)
    columns = shape_cols[0]
    positions = jnp.clip(columns - myself + REACH, 0, 2 * REACH)
    present = columns >= 0
    selected = jnp.take(window, positions, axis=0)
    selected = jnp.where(present[:, None, None], selected, jnp.zeros_like(selected))
    blocks = integrals[0]
    ladder = jnp.einsum(
        "sin,snb->ib",
        selected,
        lax.all_gather(blocks, "pair", axis=1, tiled=True),
        preferred_element_type=jnp.float32,
    )
    return (residual_in[0] + ladder)[None]


def solution(mesh):
    in_specs = (
        P("tile", "pair", None),
        P("tile", None, "pair", None),
        P("tile", "pair", None),
        P("tile", None),
    )
    out_specs = P("tile", "pair", None)
    return jax.shard_map(shards, mesh=mesh, in_specs=in_specs, out_specs=out_specs, check_vma=False)
```

profile of v0, /device:TPU:6, one launch (start us, length us, event | category | flops | bytes accessed | tf_op | source)
XLA Modules:
  0.0 117.5 jit_solution(16070119305735220322)
XLA Ops:
  6.5 0.0 copy-start
  6.5 0.0 all-gather.3.cloned.1.call-start
  6.5 0.7 all-gather.3.cloned.1.call-update
  7.3 1.9 %collective-permute-start = (bf16[768,1024]{1,0:T(8,128)(2,1)}, bf16[768,1024]{1,0:T(8,128)(2,1)}, u32[]{:S(2)}, u32[]{:S(2)}) collective-permute-start(bf16[768,1024]{1,0:T(8,128)(2,1)} %bitcast.30), channel_id=1, source_target_pairs={{0,4},{4,8},{8,12},{12,16},{16,20},{20,24},{24,28},{28,32},{32,36}... | collective-permute-start | bytes 4718600 | tf_op jit(solution)/shard_map/ppermute | solution.py:12
  9.2 7.5 %collective-permute-start.2 = (bf16[768,1024]{1,0:T(8,128)(2,1)}, bf16[768,1024]{1,0:T(8,128)(2,1)S(1)}, u32[]{:S(2)}, u32[]{:S(2)}) collective-permute-start(bf16[768,1024]{1,0:T(8,128)(2,1)} %bitcast.31), channel_id=1, source_target_pairs={{4,0},{8,4},{12,8},{16,12},{20,16},{24,20},{28,24},{32,28},{36,32}... | collective-permute-start | bytes 4718600 | tf_op jit(solution)/shard_map/ppermute | solution.py:12
  16.7 16.5 %collective-permute-done = bf16[768,1024]{1,0:T(8,128)(2,1)} collective-permute-done((bf16[768,1024]{1,0:T(8,128)(2,1)}, bf16[768,1024]{1,0:T(8,128)(2,1)}, u32[]{:S(2)}, u32[]{:S(2)}) %collective-permute-start) | collective-permute-done | bytes 1572896 | tf_op jit(solution)/shard_map/ppermute | solution.py:12
  33.1 1.9 %collective-permute-start.1 = (bf16[768,1024]{1,0:T(8,128)(2,1)}, bf16[768,1024]{1,0:T(8,128)(2,1)}, u32[]{:S(2)}, u32[]{:S(2)}) collective-permute-start(bf16[768,1024]{1,0:T(8,128)(2,1)} %collective-permute-done), channel_id=1, source_target_pairs={{0,4},{4,8},{8,12},{12,16},{16,20},{20,24},{24,28},{28,32},{32,36}... | collective-permute-start | bytes 4718600 | tf_op jit(solution)/shard_map/ppermute | solution.py:12
  35.1 0.7 fusion.13
  35.7 0.0 collective-permute-done.2
  35.7 5.7 %collective-permute-start.3 = (bf16[768,1024]{1,0:T(8,128)(2,1)S(1)}, bf16[768,1024]{1,0:T(8,128)(2,1)S(1)}, u32[]{:S(2)}, u32[]{:S(2)}) collective-permute-start(bf16[768,1024]{1,0:T(8,128)(2,1)S(1)} %collective-permute-done.2), channel_id=1, source_target_pairs={{4,0},{8,4},{12,8},{16,12},{20,16},{24,20},{28,24},{32,28},{36,32}... | collective-permute-start | bytes 4718600 | tf_op jit(solution)/shard_map/ppermute | solution.py:12
  41.5 0.7 compare_and_fusion
  42.2 0.7 compare_bitcast_fusion
  42.8 14.5 %collective-permute-done.1 = bf16[768,1024]{1,0:T(8,128)(2,1)} collective-permute-done((bf16[768,1024]{1,0:T(8,128)(2,1)}, bf16[768,1024]{1,0:T(8,128)(2,1)}, u32[]{:S(2)}, u32[]{:S(2)}) %collective-permute-start.1) | collective-permute-done | bytes 1572896 | tf_op jit(solution)/shard_map/ppermute | solution.py:12
  57.3 2.7 %bitcast_dynamic-update-slice_fusion.3 = bf16[5,768,1024]{2,1,0:T(8,128)(2,1)} fusion(bf16[768,1024]{1,0:T(8,128)(2,1)} %collective-permute-done.1), kind=kLoop, calls=%fused_computation.14 | loop fusion | bytes 3145728
  60.0 2.7 %bitcast_dynamic-update-slice_fusion.2 = bf16[5,768,1024]{2,1,0:T(8,128)(2,1)} fusion(bf16[5,768,1024]{2,1,0:T(8,128)(2,1)} %bitcast_dynamic-update-slice_fusion.3, bf16[768,1024]{1,0:T(8,128)(2,1)} %collective-permute-done), kind=kLoop, calls=%fused_computation.13 | loop fusion | bytes 3145728
  62.7 0.0 copy-done
  62.7 1.3 %constant_dynamic-update-slice_fusion = bf16[5,768,1024]{2,1,0:T(8,128)(2,1)} fusion(bf16[5,768,1024]{2,1,0:T(8,128)(2,1)} %bitcast_dynamic-update-slice_fusion.2, bf16[1,768,1024]{2,1,0:T(8,128)(2,1)S(1)} %copy-done), kind=kLoop, calls=%fused_computation.15 | loop fusion | bytes 3145728
  64.0 1.3 %bitcast_dynamic-update-slice_fusion.1 = bf16[5,768,1024]{2,1,0:T(8,128)(2,1)} fusion(bf16[5,768,1024]{2,1,0:T(8,128)(2,1)} %constant_dynamic-update-slice_fusion, bf16[768,1024]{1,0:T(8,128)(2,1)S(1)} %collective-permute-done.2), kind=kLoop, calls=%fused_computation.12 | loop fusion | bytes 3145728
  65.3 0.0 collective-permute-done.3
  65.3 1.3 %bitcast_dynamic-update-slice_fusion = bf16[5,768,1024]{2,1,0:T(8,128)(2,1)} fusion(bf16[5,768,1024]{2,1,0:T(8,128)(2,1)} %bitcast_dynamic-update-slice_fusion.1, bf16[768,1024]{1,0:T(8,128)(2,1)S(1)} %collective-permute-done.3), kind=kLoop, calls=%fused_computation.11 | loop fusion | bytes 3145728 | tf_op jit(solution)/shard_map/stack | solution.py:29
  66.6 6.8 %gather_fusion = bf16[4,768,1024]{2,1,0:T(8,128)(2,1)} fusion(bf16[5,768,1024]{2,1,0:T(8,128)(2,1)} %bitcast_dynamic-update-slice_fusion, s32[1024]{0:T(1024)S(1)} %pad_clamp_fusion), kind=kCustom, calls=%fused_computation | custom fusion | bytes 12582928 | tf_op jit(solution)/shard_map/jit(_take)/gather | solution.py:33
  73.4 24.3 %all-gather.3.cloned.1.call-done = bf16[1,4,1024,1024]{3,2,1,0:T(8,128)(2,1)} async-done(((bf16[1,4,256,1024]{3,2,1,0:T(8,128)(2,1)}), bf16[1,4,1024,1024]{3,2,1,0:T(8,128)(2,1)}) %all-gather.3.cloned.1.call-update) | async-done | bytes 8388624 | tf_op jit(solution)/shard_map/all_gather | solution.py:39
  97.8 12.9 %fusion.6 = f32[1,768,1024]{2,1,0:T(8,128)} fusion(f32[1,768,1024]{2,1,0:T(8,128)} %param.6, bf16[1,4,1024,1024]{3,2,1,0:T(8,128)(2,1)} %all-gather.3.cloned.1.call-done, bf16[4,768,1024]{2,1,0:T(8,128)(2,1)} %gather_fusion, pred[4]{0:T(512)(128)(4,1)S(1)} %compare_and_fusion, pred[4]{0:T(512)(128)(4,1)S(1)} %compare_bitcast_fusion), kind=kOutput, calls=%fused_computation.8 | convolution fusion | flops 6449528832 | bytes 20971528 | tf_op jit(solution)/shard_map/sin,snb->ib/dot_general | solution.py:36
  (1 shorter events, 0.0 us)
Async XLA Ops:
  6.5 56.2 %copy-start = (bf16[1,768,1024]{2,1,0:T(8,128)(2,1)S(1)}, bf16[1,768,1024]{2,1,0:T(8,128)(2,1)}, u32[]{:S(2)}) copy-start(bf16[1,768,1024]{2,1,0:T(8,128)(2,1)} %param.4) | copy-start | bytes 4718596
  6.5 91.2 %all-gather.3.cloned.1.call-start = ((), (), s32[]{:S(2)}) async-start(), calls=%async_computation | async-start | bytes 10485760 | tf_op jit(solution)/shard_map/all_gather | solution.py:39
  7.3 25.9 %collective-permute-start = (bf16[768,1024]{1,0:T(8,128)(2,1)}, bf16[768,1024]{1,0:T(8,128)(2,1)}, u32[]{:S(2)}, u32[]{:S(2)}) collective-permute-start(bf16[768,1024]{1,0:T(8,128)(2,1)} %bitcast.30), channel_id=1, source_target_pairs={{0,4},{4,8},{8,12},{12,16},{16,20},{20,24},{24,28},{28,32},{32,36}... | collective-permute-start | bytes 4718600 | tf_op jit(solution)/shard_map/ppermute | solution.py:12
  9.2 26.5 %collective-permute-start.2 = (bf16[768,1024]{1,0:T(8,128)(2,1)}, bf16[768,1024]{1,0:T(8,128)(2,1)S(1)}, u32[]{:S(2)}, u32[]{:S(2)}) collective-permute-start(bf16[768,1024]{1,0:T(8,128)(2,1)} %bitcast.31), channel_id=1, source_target_pairs={{4,0},{8,4},{12,8},{16,12},{20,16},{24,20},{28,24},{32,28},{36,32}... | collective-permute-start | bytes 4718600 | tf_op jit(solution)/shard_map/ppermute | solution.py:12
  33.1 24.1 %collective-permute-start.1 = (bf16[768,1024]{1,0:T(8,128)(2,1)}, bf16[768,1024]{1,0:T(8,128)(2,1)}, u32[]{:S(2)}, u32[]{:S(2)}) collective-permute-start(bf16[768,1024]{1,0:T(8,128)(2,1)} %collective-permute-done), channel_id=1, source_target_pairs={{0,4},{4,8},{8,12},{12,16},{16,20},{20,24},{24,28},{28,32},{32,36}... | collective-permute-start | bytes 4718600 | tf_op jit(solution)/shard_map/ppermute | solution.py:12
  35.7 29.6 %collective-permute-start.3 = (bf16[768,1024]{1,0:T(8,128)(2,1)S(1)}, bf16[768,1024]{1,0:T(8,128)(2,1)S(1)}, u32[]{:S(2)}, u32[]{:S(2)}) collective-permute-start(bf16[768,1024]{1,0:T(8,128)(2,1)S(1)} %collective-permute-done.2), channel_id=1, source_target_pairs={{4,0},{8,4},{12,8},{16,12},{20,16},{24,20},{28,24},{32,28},{36,32}... | collective-permute-start | bytes 4718600 | tf_op jit(solution)/shard_map/ppermute | solution.py:12
Sparse Core Ops, SparseCore 0:
  9.2 88.5 all-gather.2
where the time goes:
time: 119 us; the launch traced here: 118 us
  waiting for transfers between devices  56 us (47%)
  starting transfers between devices  17 us (14%)
  local copies, waits for them, and re-layouts  16.2 us (14%)
  between operations  13.4 us (11%)
  matrix products  12.9 us (11%)
  other arithmetic  2 us (2%)
    ppermute x4, waiting for transfers between devices, shifted(): return lax.ppermute(block, axis, route)  30.9 us
    all_gather x1, waiting for transfers between devices, shards(): lax.all_gather(blocks, 'pair', axis=1, tiled=True)  24.3 us
    ppermute x4, starting transfers between devices, shifted(): return lax.ppermute(block, axis, route)  17 us
    dot_general x1, matrix products, shards(): jnp.einsum('sin,snb->ib', selected, lax.all_gather(blocks, 'pair', axis=1...  12.9 us
    unnamed x6, local copies, waits for them, and re-layouts  8.03 us
    gather x1, local copies, waits for them, and re-layouts, shards(): selected = jnp.take(window, positions, axis=0)  6.85 us
  transfers between devices with their start and end apart: 5, of which 3 were waited for; matrix products, arithmetic and copies ran while one was open for 15% of the time, Pallas kernels for 0%

commit v1 on v0

v1 whole, which is shorter than its diff:
```python
import jax
import jax.numpy as jnp
from jax import lax
from jax.experimental import pallas as pl
from jax.experimental.pallas import tpu as pltpu
from jax.sharding import PartitionSpec as P

REACH = 2
SLOTS = 4
MIB = 1024 * 1024
VMEM = pl.BlockSpec(memory_space=pltpu.VMEM)
SMEM = pl.BlockSpec(memory_space=pltpu.SMEM)
ANY = pl.BlockSpec(memory_space=pl.ANY)


def shifted(block, axis, distance):
    devices = range(lax.axis_size(axis))
    route = [(i - distance, i) for i in devices if i - distance in devices]
    return lax.ppermute(block, axis, route)


def turned(block, axis, distance):
    size = lax.axis_size(axis)
    return lax.ppermute(block, axis, [(i, (i + distance) % size) for i in range(size)])


def near_kernel(below, above, mine, low2, low1, own, high1, high2, residual, listed, total, kept, chosen):
    rows = residual.shape[0]
    width = mine.shape[1]
    myself = lax.axis_index("tile")
    pair = lax.axis_index("pair")
    nothing = jnp.where(myself < REACH, 0, 2 * REACH)

    for slot in range(SLOTS):
        column = listed[0, slot]
        place = jnp.where(column >= 0, jnp.clip(column - myself + REACH, 0, 2 * REACH), nothing)
        for index, source in enumerate((low2, low1, own, high1, high2)):

            @pl.when(place == index)
            def _():
                for turn, step in enumerate((0, -1, 1, 2)):
                    begin = pl.multiple_of(lax.rem(pair + 4 + step, 4) * width, width)
                    part = source[:, pl.ds(begin, width)]
                    if turn < 3:
                        chosen[turn, :, slot * width : (slot + 1) * width] = part
                    else:
                        kept[:, slot * width : (slot + 1) * width] = part

    lanes = 256
    for begin in range(0, residual.shape[1], lanes):
        value = residual[:, begin : begin + lanes]
        for turn, shard in enumerate((mine, below, above)):
            right = shard[:, :, begin : begin + lanes].reshape(SLOTS * width, lanes)
            value += jnp.dot(chosen[turn], right, preferred_element_type=jnp.float32)
        total[:, begin : begin + lanes] = value


def far_kernel(first, second, total, kept, out, staged, sems):
    width = first.shape[1]
    half = first.shape[0] * width
    lanes = 256
    copies = []
    for tile in range(total.shape[1] // lanes):
        here = slice(tile * lanes, (tile + 1) * lanes)
        value = jnp.dot(kept[:, :half], first[:, :, here].reshape(half, lanes), preferred_element_type=jnp.float32)
        value += jnp.dot(kept[:, half:], second[:, :, here].reshape(half, lanes), preferred_element_type=jnp.float32)
        staged[:, here] = total[:, here] + value
        copies.append(pltpu.make_async_copy(staged.at[:, here], out.at[:, here], sems.at[tile]))
        copies[-1].start()
    for copy in copies:
        copy.wait()


def pass_kernel(*refs):
    del refs


def passed(blocks, flops):
    count = len(blocks)
    return pl.pallas_call(
        pass_kernel,
        out_shape=[jax.ShapeDtypeStruct(block.shape, block.dtype) for block in blocks],
        in_specs=[ANY] * count,
        out_specs=[ANY] * count,
        input_output_aliases={index: index for index in range(count)},
        compiler_params=pltpu.CompilerParams(vmem_limit_bytes=MIB),
        cost_estimate=pl.CostEstimate(flops=flops, bytes_accessed=0, transcendentals=0),
    )(*blocks)


def shards(amplitudes, integrals, residual_in, shape_cols):
    own = amplitudes[0]
    mine = integrals[0]
    width, columns = mine.shape[1], mine.shape[2]
    rows = own.shape[0]

    below = turned(mine, "pair", 1)
    above = turned(mine, "pair", -1)
    low1 = shifted(own, "tile", 1)
    high1 = shifted(own, "tile", -1)
    low2 = shifted(low1, "tile", 1)
    high2 = shifted(high1, "tile", -1)
    below, above = passed((below, above), 20000000000)
    far_first = turned(below[:2], "pair", 1)
    far_second = turned(above[2:], "pair", -1)

    total, kept = pl.pallas_call(
        near_kernel,
        out_shape=[
            jax.ShapeDtypeStruct((rows, columns), jnp.float32),
            jax.ShapeDtypeStruct((rows, SLOTS * width), own.dtype),
        ],
        in_specs=[VMEM] * 9 + [SMEM],
        out_specs=[VMEM] * 2,
        scratch_shapes=[pltpu.VMEM((3, rows, SLOTS * width), own.dtype)],
        compiler_params=pltpu.CompilerParams(vmem_limit_bytes=16 * MIB),
        cost_estimate=pl.CostEstimate(flops=1 << 32, bytes_accessed=1 << 20, transcendentals=0),
    )(below, above, mine, low2, low1, own, high1, high2, residual_in[0], shape_cols)
    out = pl.pallas_call(
        far_kernel,
        out_shape=jax.ShapeDtypeStruct((rows, columns), jnp.float32),
        in_specs=[VMEM] * 4,
        out_specs=ANY,
        scratch_shapes=[pltpu.VMEM((rows, columns), jnp.float32), pltpu.SemaphoreType.DMA((4,))],
        compiler_params=pltpu.CompilerParams(vmem_limit_bytes=12 * MIB),
        cost_estimate=pl.CostEstimate(flops=1 << 30, bytes_accessed=1 << 20, transcendentals=0),
    )(far_first, far_second, total, kept)
    return out[None]


def solution(mesh):
    in_specs = (
        P("tile", "pair", None),
        P("tile", None, "pair", None),
        P("tile", "pair", None),
        P("tile", None),
    )
    out_specs = P("tile", "pair", None)
    return jax.shard_map(shards, mesh=mesh, in_specs=in_specs, out_specs=out_specs, check_vma=False)
```

time: 119 us -> 80.2 us (0.67); the launches traced: 118 us -> 80 us
  local copies, waits for them, and re-layouts: 16.2 us -> 0.15 us
  between operations: 13.4 us -> 0.25 us
  matrix products: 12.9 us -> 0 us
  Pallas kernels: 0 us -> 9.88 us
  waiting for transfers between devices: 56 us -> 46.6 us
  starting transfers between devices: 17 us -> 23.1 us
  other arithmetic: 2 us -> 0 us
    ppermute x0 -> x4, waiting for transfers between devices: none -> 27.2 us  [turned(): lax.ppermute(block, axis, [(i, (i + distance) % size) for i in range(size)])]
    all_gather x1 -> x0, waiting for transfers between devices: 24.3 us -> none  [shards(): lax.all_gather(blocks, 'pair', axis=1, tiled=True)]
    dot_general x1 -> x0, matrix products: 12.9 us -> none  [shards(): jnp.einsum('sin,snb->ib', selected, lax.all_gather(blocks, 'pair', axis=1...]
    ppermute x4, waiting for transfers between devices: 30.9 us -> 19.4 us  [shifted(): return lax.ppermute(block, axis, route)]
    pallas_call x0 -> x3, Pallas kernels: none -> 9.88 us  [the longest x1 6.71 us: shards(): pl.pallas_call(near_kernel, out_shape=[jax.ShapeDtypeStruct((rows, column...]
    unnamed x6 -> x8, local copies, waits for them, and re-layouts: 8.03 us -> 0.01 us
    gather x1 -> x0, local copies, waits for them, and re-layouts: 6.85 us -> none  [shards(): selected = jnp.take(window, positions, axis=0)]
    ppermute x0 -> x4, starting transfers between devices: none -> 6.32 us  [turned(): lax.ppermute(block, axis, [(i, (i + distance) % size) for i in range(size)])]
  transfers between devices with their start and end apart: 5 -> 8, of which waited for: 3 -> 5; matrix products, arithmetic and copies ran while one was open for 15% -> 0% of each run, Pallas kernels for 0% -> 8%
where the time goes in v1:
time: 80.2 us; the launch traced here: 80 us
  waiting for transfers between devices  46.6 us (58%)
  starting transfers between devices  23.1 us (29%)
  Pallas kernels  9.88 us (12%)
    ppermute x4, waiting for transfers between devices, turned(): lax.ppermute(block, axis, [(i, (i + distance) % size) for i in range(size)])  27.2 us
    ppermute x4, waiting for transfers between devices, shifted(): return lax.ppermute(block, axis, route)  19.4 us
    ppermute x4, starting transfers between devices, shifted(): return lax.ppermute(block, axis, route)  16.8 us
    pallas_call x1, Pallas kernels, shards(): pl.pallas_call(near_kernel, out_shape=[jax.ShapeDtypeStruct((rows, column...  6.71 us
    ppermute x4, starting transfers between devices, turned(): lax.ppermute(block, axis, [(i, (i + distance) % size) for i in range(size)])  6.32 us
    pallas_call x1, Pallas kernels, shards(): pl.pallas_call(far_kernel, out_shape=jax.ShapeDtypeStruct((rows, columns)...  3.18 us
  transfers between devices with their start and end apart: 8, of which 5 were waited for; matrix products, arithmetic and copies ran while one was open for 0% of the time, Pallas kernels for 8%

profile of v1, /device:TPU:6, one launch (start us, length us, event | category | flops | bytes accessed | tf_op | source)
XLA Modules:
  0.0 80.0 jit_solution(2100514330036332922)
XLA Ops:
  0.0 3.0 %collective-permute-start.1 = (bf16[4,256,1024]{2,1,0:T(8,128)(2,1)}, bf16[4,256,1024]{2,1,0:T(8,128)(2,1)S(1)}, u32[]{:S(2)}, u32[]{:S(2)}) collective-permute-start(bf16[4,256,1024]{2,1,0:T(8,128)(2,1)} %bitcast.5), channel_id=1, source_target_pairs={{0,3},{1,0},{2,1},{3,2},{4,7},{5,4},{6,5},{7,6},{8,11},{9,8},{10,9... | collective-permute-start | bytes 6291464 | tf_op jit(solution)/shard_map/ppermute | solution.py:24
  3.0 0.0 collective-permute-start
  3.0 7.2 %collective-permute-start.6 = (bf16[768,1024]{1,0:T(8,128)(2,1)}, bf16[768,1024]{1,0:T(8,128)(2,1)S(1)}, u32[]{:S(2)}, u32[]{:S(2)}) collective-permute-start(bf16[768,1024]{1,0:T(8,128)(2,1)} %bitcast.8), channel_id=1, source_target_pairs={{4,0},{8,4},{12,8},{16,12},{20,16},{24,20},{28,24},{32,28},{36,32}... | collective-permute-start | bytes 4718600 | tf_op jit(solution)/shard_map/ppermute | solution.py:19
  10.2 1.9 %collective-permute-start.4 = (bf16[768,1024]{1,0:T(8,128)(2,1)}, bf16[768,1024]{1,0:T(8,128)(2,1)S(1)}, u32[]{:S(2)}, u32[]{:S(2)}) collective-permute-start(bf16[768,1024]{1,0:T(8,128)(2,1)} %bitcast.9), channel_id=1, source_target_pairs={{0,4},{4,8},{8,12},{12,16},{16,20},{20,24},{24,28},{28,32},{32,36}... | collective-permute-start | bytes 4718600 | tf_op jit(solution)/shard_map/ppermute | solution.py:19
  12.1 16.3 %collective-permute-done.6.high1 = bf16[768,1024]{1,0:T(8,128)(2,1)S(1)} collective-permute-done((bf16[768,1024]{1,0:T(8,128)(2,1)}, bf16[768,1024]{1,0:T(8,128)(2,1)S(1)}, u32[]{:S(2)}, u32[]{:S(2)}) %collective-permute-start.6) | collective-permute-done | bytes 1572896 | tf_op jit(solution)/shard_map/ppermute | solution.py:19
  28.4 5.8 %collective-permute-start.7 = (bf16[768,1024]{1,0:T(8,128)(2,1)S(1)}, bf16[768,1024]{1,0:T(8,128)(2,1)S(1)}, u32[]{:S(2)}, u32[]{:S(2)}) collective-permute-start(bf16[768,1024]{1,0:T(8,128)(2,1)S(1)} %collective-permute-done.6.high1), channel_id=1, source_target_pairs={{4,0},{8,4},{12,8},{16,12},{20,16},{24,20},{28,24},{32,28},{36,32}... | collective-permute-start | bytes 4718600 | tf_op jit(solution)/shard_map/ppermute | solution.py:19
  34.2 0.0 collective-permute-done.4.low1
  34.3 1.9 %collective-permute-start.5 = (bf16[768,1024]{1,0:T(8,128)(2,1)S(1)}, bf16[768,1024]{1,0:T(8,128)(2,1)S(1)}, u32[]{:S(2)}, u32[]{:S(2)}) collective-permute-start(bf16[768,1024]{1,0:T(8,128)(2,1)S(1)} %collective-permute-done.4.low1), channel_id=1, source_target_pairs={{0,4},{4,8},{8,12},{12,16},{16,20},{20,24},{24,28},{28,32},{32,36}... | collective-permute-start | bytes 4718600 | tf_op jit(solution)/shard_map/ppermute | solution.py:19
  36.2 12.0 %collective-permute-done.1.refs_1_ = bf16[4,256,1024]{2,1,0:T(8,128)(2,1)S(1)} collective-permute-done((bf16[4,256,1024]{2,1,0:T(8,128)(2,1)}, bf16[4,256,1024]{2,1,0:T(8,128)(2,1)S(1)}, u32[]{:S(2)}, u32[]{:S(2)}) %collective-permute-start.1) | collective-permute-done | bytes 2097184 | tf_op jit(solution)/shard_map/ppermute | solution.py:24
  48.2 3.3 %collective-permute-done.refs_0_ = bf16[4,256,1024]{2,1,0:T(8,128)(2,1)S(1)} collective-permute-done((bf16[4,256,1024]{2,1,0:T(8,128)(2,1)}, bf16[4,256,1024]{2,1,0:T(8,128)(2,1)S(1)}, u32[]{:S(2)}, u32[]{:S(2)}) %collective-permute-start) | collective-permute-done | bytes 2097184 | tf_op jit(solution)/shard_map/ppermute | solution.py:24
  51.5 0.1 slice.7
  51.6 0.1 slice.6
  51.7 0.1 collective-permute-start.2
  51.8 3.2 %collective-permute-start.3 = (bf16[2,256,1024]{2,1,0:T(8,128)(2,1)S(1)}, bf16[2,256,1024]{2,1,0:T(8,128)(2,1)S(1)}, u32[]{:S(2)}, u32[]{:S(2)}) collective-permute-start(bf16[2,256,1024]{2,1,0:T(8,128)(2,1)S(1)} %slice.7), channel_id=1, source_target_pairs={{0,3},{1,0},{2,1},{3,2},{4,7},{5,4},{6,5},{7,6},{8,11},{9,8},{10,9... | collective-permute-start | bytes 3145736 | tf_op jit(solution)/shard_map/ppermute | solution.py:24
  55.0 0.0 collective-permute-done.7.high2
  55.0 3.1 %collective-permute-done.5.low2 = bf16[768,1024]{1,0:T(8,128)(2,1)S(1)} collective-permute-done((bf16[768,1024]{1,0:T(8,128)(2,1)S(1)}, bf16[768,1024]{1,0:T(8,128)(2,1)S(1)}, u32[]{:S(2)}, u32[]{:S(2)}) %collective-permute-start.5) | collective-permute-done | bytes 1572896 | tf_op jit(solution)/shard_map/ppermute | solution.py:19
  58.1 0.0 copy-done.1
  58.1 0.0 copy-done.2
  58.1 0.0 copy-done
  58.1 0.0 copy-done.3
  58.1 6.7 %shard_map.47 = (f32[768,1024]{1,0:T(8,128)S(1)}, bf16[768,1024]{1,0:T(8,128)(2,1)S(1)}) custom-call(bf16[4,256,1024]{2,1,0:T(8,128)(2,1)S(1)} %get-tuple-element.9.below, bf16[4,256,1024]{2,1,0:T(8,128)(2,1)S(1)} %get-tuple-element.10.above, bf16[4,256,1024]{2,1,0:T(8,128)(2,1)S(1)} %bitcast.7, bf16[768,1024]{1,0:T(8,128)(2,1)S(1)} %collective-permute-done.5.low2, ...), custom_call_target="tpu_custom_call" | custom-call | flops 4294967296 | bytes 1048576 | tf_op jit(solution)/shard_map/pallas_call | solution.py:107
  64.8 11.9 %collective-permute-done.2.first = bf16[2,256,1024]{2,1,0:T(8,128)(2,1)S(1)} collective-permute-done((bf16[2,256,1024]{2,1,0:T(8,128)(2,1)S(1)}, bf16[2,256,1024]{2,1,0:T(8,128)(2,1)S(1)}, u32[]{:S(2)}, u32[]{:S(2)}) %collective-permute-start.2) | collective-permute-done | bytes 1048608 | tf_op jit(solution)/shard_map/ppermute | solution.py:24
  76.7 0.0 collective-permute-done.3.second
  76.7 3.2 %shard_map.48 = f32[768,1024]{1,0:T(8,128)} custom-call(bf16[2,256,1024]{2,1,0:T(8,128)(2,1)S(1)} %collective-permute-done.2.first, bf16[2,256,1024]{2,1,0:T(8,128)(2,1)S(1)} %collective-permute-done.3.second, f32[768,1024]{1,0:T(8,128)S(1)} %get-tuple-element.11.total, bf16[768,1024]{1,0:T(8,128)(2,1)S(1)} %get-tuple-element.12.kept), custom_call_target="tpu_custom_call" | custom-call | flops 1073741824 | bytes 1048576 | tf_op jit(solution)/shard_map/pallas_call | solution.py:119
  (5 shorter events, 0.0 us)
Async XLA Ops:
  0.0 48.2 %collective-permute-start.1 = (bf16[4,256,1024]{2,1,0:T(8,128)(2,1)}, bf16[4,256,1024]{2,1,0:T(8,128)(2,1)S(1)}, u32[]{:S(2)}, u32[]{:S(2)}) collective-permute-start(bf16[4,256,1024]{2,1,0:T(8,128)(2,1)} %bitcast.5), channel_id=1, source_target_pairs={{0,3},{1,0},{2,1},{3,2},{4,7},{5,4},{6,5},{7,6},{8,11},{9,8},{10,9... | collective-permute-start | bytes 6291464 | tf_op jit(solution)/shard_map/ppermute | solution.py:24
  3.0 48.5 %collective-permute-start = (bf16[4,256,1024]{2,1,0:T(8,128)(2,1)}, bf16[4,256,1024]{2,1,0:T(8,128)(2,1)S(1)}, u32[]{:S(2)}, u32[]{:S(2)}) collective-permute-start(bf16[4,256,1024]{2,1,0:T(8,128)(2,1)} %bitcast.6), channel_id=1, source_target_pairs={{0,1},{1,2},{2,3},{3,0},{4,5},{5,6},{6,7},{7,4},{8,9},{9,10},{10,1... | collective-permute-start | bytes 6291464 | tf_op jit(solution)/shard_map/ppermute | solution.py:24
  3.0 25.4 %collective-permute-start.6 = (bf16[768,1024]{1,0:T(8,128)(2,1)}, bf16[768,1024]{1,0:T(8,128)(2,1)S(1)}, u32[]{:S(2)}, u32[]{:S(2)}) collective-permute-start(bf16[768,1024]{1,0:T(8,128)(2,1)} %bitcast.8), channel_id=1, source_target_pairs={{4,0},{8,4},{12,8},{16,12},{20,16},{24,20},{28,24},{32,28},{36,32}... | collective-permute-start | bytes 4718600 | tf_op jit(solution)/shard_map/ppermute | solution.py:19
  10.2 24.1 %collective-permute-start.4 = (bf16[768,1024]{1,0:T(8,128)(2,1)}, bf16[768,1024]{1,0:T(8,128)(2,1)S(1)}, u32[]{:S(2)}, u32[]{:S(2)}) collective-permute-start(bf16[768,1024]{1,0:T(8,128)(2,1)} %bitcast.9), channel_id=1, source_target_pairs={{0,4},{4,8},{8,12},{12,16},{16,20},{20,24},{24,28},{28,32},{32,36}... | collective-permute-start | bytes 4718600 | tf_op jit(solution)/shard_map/ppermute | solution.py:19
  28.4 26.6 %collective-permute-start.7 = (bf16[768,1024]{1,0:T(8,128)(2,1)S(1)}, bf16[768,1024]{1,0:T(8,128)(2,1)S(1)}, u32[]{:S(2)}, u32[]{:S(2)}) collective-permute-start(bf16[768,1024]{1,0:T(8,128)(2,1)S(1)} %collective-permute-done.6.high1), channel_id=1, source_target_pairs={{4,0},{8,4},{12,8},{16,12},{20,16},{24,20},{28,24},{32,28},{36,32}... | collective-permute-start | bytes 4718600 | tf_op jit(solution)/shard_map/ppermute | solution.py:19
  34.3 23.8 %collective-permute-start.5 = (bf16[768,1024]{1,0:T(8,128)(2,1)S(1)}, bf16[768,1024]{1,0:T(8,128)(2,1)S(1)}, u32[]{:S(2)}, u32[]{:S(2)}) collective-permute-start(bf16[768,1024]{1,0:T(8,128)(2,1)S(1)} %collective-permute-done.4.low1), channel_id=1, source_target_pairs={{0,4},{4,8},{8,12},{12,16},{16,20},{20,24},{24,28},{28,32},{32,36}... | collective-permute-start | bytes 4718600 | tf_op jit(solution)/shard_map/ppermute | solution.py:19
  51.5 6.6 %copy-start.1 = (bf16[1,4,256,1024]{3,2,1,0:T(8,128)(2,1)S(1)}, bf16[1,4,256,1024]{3,2,1,0:T(8,128)(2,1)}, u32[]{:S(2)}) copy-start(bf16[1,4,256,1024]{3,2,1,0:T(8,128)(2,1)} %param.5) | copy-start | bytes 6291460
  51.5 6.6 %copy-start.2 = (bf16[1,768,1024]{2,1,0:T(8,128)(2,1)S(1)}, bf16[1,768,1024]{2,1,0:T(8,128)(2,1)}, u32[]{:S(2)}) copy-start(bf16[1,768,1024]{2,1,0:T(8,128)(2,1)} %param.4) | copy-start | bytes 4718596
  51.5 6.6 %copy-start = (f32[1,768,1024]{2,1,0:T(8,128)S(1)}, f32[1,768,1024]{2,1,0:T(8,128)}, u32[]{:S(2)}) copy-start(f32[1,768,1024]{2,1,0:T(8,128)} %param.6) | copy-start | bytes 9437188
  51.5 6.6 %copy-start.3 = (s32[1,4]{1,0:T(1,128)S(1)}, s32[1,4]{1,0:T(1,128)}, u32[]{:S(2)}) copy-start(s32[1,4]{1,0:T(1,128)} %listed.1) | copy-start | bytes 52
  51.7 25.0 %collective-permute-start.2 = (bf16[2,256,1024]{2,1,0:T(8,128)(2,1)S(1)}, bf16[2,256,1024]{2,1,0:T(8,128)(2,1)S(1)}, u32[]{:S(2)}, u32[]{:S(2)}) collective-permute-start(bf16[2,256,1024]{2,1,0:T(8,128)(2,1)S(1)} %slice.6), channel_id=1, source_target_pairs={{0,1},{1,2},{2,3},{3,0},{4,5},{5,6},{6,7},{7,4},{8,9},{9,10},{10,1... | collective-permute-start | bytes 3145736 | tf_op jit(solution)/shard_map/ppermute | solution.py:24
  51.8 24.9 %collective-permute-start.3 = (bf16[2,256,1024]{2,1,0:T(8,128)(2,1)S(1)}, bf16[2,256,1024]{2,1,0:T(8,128)(2,1)S(1)}, u32[]{:S(2)}, u32[]{:S(2)}) collective-permute-start(bf16[2,256,1024]{2,1,0:T(8,128)(2,1)S(1)} %slice.7), channel_id=1, source_target_pairs={{0,3},{1,0},{2,1},{3,2},{4,7},{5,4},{6,5},{7,6},{8,11},{9,8},{10,9... | collective-permute-start | bytes 3145736 | tf_op jit(solution)/shard_map/ppermute | solution.py:24

commit v2 on v1

--- a/solution.py
+++ b/solution.py
@@ -1,3 +1,5 @@
+import functools
+
 import jax
 import jax.numpy as jnp
 from jax import lax
@@ -7,6 +9,7 @@
 
 REACH = 2
 SLOTS = 4
+FRONT = 768
 MIB = 1024 * 1024
 VMEM = pl.BlockSpec(memory_space=pltpu.VMEM)
 SMEM = pl.BlockSpec(memory_space=pltpu.SMEM)
@@ -55,37 +58,43 @@
         total[:, begin : begin + lanes] = value
 
 
-def far_kernel(first, second, total, kept, out, staged, sems):
-    width = first.shape[1]
-    half = first.shape[0] * width
+def split_kernel(below, above, *pieces):
+    half = SLOTS // 2
+    for source, begin, (front, back) in ((below, 0, pieces[:2]), (above, half, pieces[2:])):
+        front[...] = source[begin : begin + half, :, :FRONT]
+        back[...] = source[begin : begin + half, :, FRONT:]
+
+
+def far_kernel(begin, first, second, total, kept, *rest):
+    out, staged, sems = rest[-3:]
+    half = first.shape[0] * first.shape[1]
     lanes = 256
     copies = []
-    for tile in range(total.shape[1] // lanes):
-        here = slice(tile * lanes, (tile + 1) * lanes)
-        value = jnp.dot(kept[:, :half], first[:, :, here].reshape(half, lanes), preferred_element_type=jnp.float32)
-        value += jnp.dot(kept[:, half:], second[:, :, here].reshape(half, lanes), preferred_element_type=jnp.float32)
-        staged[:, here] = total[:, here] + value
-        copies.append(pltpu.make_async_copy(staged.at[:, here], out.at[:, here], sems.at[tile]))
+    for tile in range(first.shape[2] // lanes):
+        piece = slice(tile * lanes, (tile + 1) * lanes)
+        here = slice(begin + tile * lanes, begin + (tile + 1) * lanes)
+        value = jnp.dot(kept[:, :half], first[:, :, piece].reshape(half, lanes), preferred_element_type=jnp.float32)
+        value += jnp.dot(kept[:, half:], second[:, :, piece].reshape(half, lanes), preferred_element_type=jnp.float32)
+        staged[:, piece] = total[:, here] + value
+        copies.append(pltpu.make_async_copy(staged.at[:, piece], out.at[:, here], sems.at[tile]))
         copies[-1].start()
     for copy in copies:
         copy.wait()
 
 
-def pass_kernel(*refs):
-    del refs
-
-
-def passed(blocks, flops):
-    count = len(blocks)
+def far_columns(begin, first, second, total, kept, *out):
+    rows = total.shape[0]
+    width = first.shape[2]
     return pl.pallas_call(
-        pass_kernel,
-        out_shape=[jax.ShapeDtypeStruct(block.shape, block.dtype) for block in blocks],
-        in_specs=[ANY] * count,
-        out_specs=[ANY] * count,
-        input_output_aliases={index: index for index in range(count)},
-        compiler_params=pltpu.CompilerParams(vmem_limit_bytes=MIB),
-        cost_estimate=pl.CostEstimate(flops=flops, bytes_accessed=0, transcendentals=0),
-    )(*blocks)
+        functools.partial(far_kernel, begin),
+        out_shape=jax.ShapeDtypeStruct(total.shape, total.dtype),
+        in_specs=[VMEM] * 4 + [ANY] * len(out),
+        out_specs=ANY,
+        input_output_aliases={4: 0} if out else {},
+        scratch_shapes=[pltpu.VMEM((rows, width), jnp.float32), pltpu.SemaphoreType.DMA((4,))],
+        compiler_params=pltpu.CompilerParams(vmem_limit_bytes=12 * MIB),
+        cost_estimate=pl.CostEstimate(flops=1 << 29, bytes_accessed=1 << 20, transcendentals=0),
+    )(first, second, total, kept, *out)
 
 
 def shards(amplitudes, integrals, residual_in, shape_cols):
@@ -100,9 +109,19 @@
     high1 = shifted(own, "tile", -1)
     low2 = shifted(low1, "tile", 1)
     high2 = shifted(high1, "tile", -1)
-    below, above = passed((below, above), 20000000000)
-    far_first = turned(below[:2], "pair", 1)
-    far_second = turned(above[2:], "pair", -1)
+    half = SLOTS // 2
+    front = jax.ShapeDtypeStruct((half, width, FRONT), mine.dtype)
+    back = jax.ShapeDtypeStruct((half, width, columns - FRONT), mine.dtype)
+    pieces = pl.pallas_call(
+        split_kernel,
+        out_shape=[front, back, front, back],
+        in_specs=[VMEM] * 2,
+        out_specs=[VMEM] * 4,
+        compiler_params=pltpu.CompilerParams(vmem_limit_bytes=4 * MIB),
+        cost_estimate=pl.CostEstimate(flops=20_000_000_000, bytes_accessed=0, transcendentals=0),
+    )(below, above)
+    first_front, second_front = turned(pieces[0], "pair", 1), turned(pieces[2], "pair", -1)
+    first_back, second_back = turned(pieces[1], "pair", 1), turned(pieces[3], "pair", -1)
 
     total, kept = pl.pallas_call(
         near_kernel,
@@ -116,15 +135,8 @@
         compiler_params=pltpu.CompilerParams(vmem_limit_bytes=16 * MIB),
         cost_estimate=pl.CostEstimate(flops=1 << 32, bytes_accessed=1 << 20, transcendentals=0),
     )(below, above, mine, low2, low1, own, high1, high2, residual_in[0], shape_cols)
-    out = pl.pallas_call(
-        far_kernel,
-        out_shape=jax.ShapeDtypeStruct((rows, columns), jnp.float32),
-        in_specs=[VMEM] * 4,
-        out_specs=ANY,
-        scratch_shapes=[pltpu.VMEM((rows, columns), jnp.float32), pltpu.SemaphoreType.DMA((4,))],
-        compiler_params=pltpu.CompilerParams(vmem_limit_bytes=12 * MIB),
-        cost_estimate=pl.CostEstimate(flops=1 << 30, bytes_accessed=1 << 20, transcendentals=0),
-    )(far_first, far_second, total, kept)
+    out = far_columns(0, first_front, second_front, total, kept)
+    out = far_columns(FRONT, first_back, second_back, total, kept, out)
     return out[None]
 
 

time: 80.2 us -> 78.5 us (0.979)
  waiting for transfers between devices: 46.6 us -> 40.4 us
  starting transfers between devices: 23.1 us -> 26.7 us
  Pallas kernels: 9.88 us -> 11 us
    ppermute x4 -> x6, starting transfers between devices: 6.32 us -> 9.56 us  [turned(): lax.ppermute(block, axis, [(i, (i + distance) % size) for i in range(size)])]
    ppermute x4 -> x6, waiting for transfers between devices: 27.2 us -> 24 us  [turned(): lax.ppermute(block, axis, [(i, (i + distance) % size) for i in range(size)])]
    ppermute x4, waiting for transfers between devices: 19.4 us -> 16.5 us  [shifted(): return lax.ppermute(block, axis, route)]
    pallas_call x2 -> x3, Pallas kernels: 3.18 us -> 4.29 us  [the longest x2 4.12 us: far_columns(): pl.pallas_call(functools.partial(far_kernel, begin), out_shape=jax.ShapeD...]
  transfers between devices with their start and end apart: 8 -> 10, of which waited for: 5 -> 6; matrix products, arithmetic and copies ran while one was open for 0% -> 0% of each run, Pallas kernels for 8% -> 12%
where the time goes in v2:
time: 78.5 us; the launch traced here: 78.3 us
  waiting for transfers between devices  40.4 us (51%)
  starting transfers between devices  26.7 us (34%)
  Pallas kernels  11 us (14%)
    ppermute x6, waiting for transfers between devices, turned(): lax.ppermute(block, axis, [(i, (i + distance) % size) for i in range(size)])  24 us
    ppermute x4, starting transfers between devices, shifted(): return lax.ppermute(block, axis, route)  17.1 us
    ppermute x4, waiting for transfers between devices, shifted(): return lax.ppermute(block, axis, route)  16.5 us
    ppermute x6, starting transfers between devices, turned(): lax.ppermute(block, axis, [(i, (i + distance) % size) for i in range(size)])  9.56 us
    pallas_call x1, Pallas kernels, shards(): pl.pallas_call(near_kernel, out_shape=[jax.ShapeDtypeStruct((rows, column...  6.71 us
    pallas_call x2, Pallas kernels, far_columns(): pl.pallas_call(functools.partial(far_kernel, begin), out_shape=jax.ShapeD...  4.12 us
  transfers between devices with their start and end apart: 10, of which 6 were waited for; matrix products, arithmetic and copies ran while one was open for 0% of the time, Pallas kernels for 12%

profile of v2, /device:TPU:6, one launch (start us, length us, event | category | flops | bytes accessed | tf_op | source)
XLA Modules:
  0.0 78.3 jit_solution(8577065786587212097)
XLA Ops:
  0.0 3.0 %collective-permute-start.1 = (bf16[4,256,1024]{2,1,0:T(8,128)(2,1)}, bf16[4,256,1024]{2,1,0:T(8,128)(2,1)S(1)}, u32[]{:S(2)}, u32[]{:S(2)}) collective-permute-start(bf16[4,256,1024]{2,1,0:T(8,128)(2,1)} %bitcast.5), channel_id=1, source_target_pairs={{0,3},{1,0},{2,1},{3,2},{4,7},{5,4},{6,5},{7,6},{8,11},{9,8},{10,9... | collective-permute-start | bytes 6291464 | tf_op jit(solution)/shard_map/ppermute | solution.py:27
  3.0 0.0 collective-permute-start
  3.0 7.5 %collective-permute-start.6 = (bf16[768,1024]{1,0:T(8,128)(2,1)}, bf16[768,1024]{1,0:T(8,128)(2,1)S(1)}, u32[]{:S(2)}, u32[]{:S(2)}) collective-permute-start(bf16[768,1024]{1,0:T(8,128)(2,1)} %bitcast.8), channel_id=1, source_target_pairs={{4,0},{8,4},{12,8},{16,12},{20,16},{24,20},{28,24},{32,28},{36,32}... | collective-permute-start | bytes 4718600 | tf_op jit(solution)/shard_map/ppermute | solution.py:22
  10.5 1.9 %collective-permute-start.4 = (bf16[768,1024]{1,0:T(8,128)(2,1)}, bf16[768,1024]{1,0:T(8,128)(2,1)S(1)}, u32[]{:S(2)}, u32[]{:S(2)}) collective-permute-start(bf16[768,1024]{1,0:T(8,128)(2,1)} %bitcast.9), channel_id=1, source_target_pairs={{0,4},{4,8},{8,12},{12,16},{16,20},{20,24},{24,28},{28,32},{32,36}... | collective-permute-start | bytes 4718600 | tf_op jit(solution)/shard_map/ppermute | solution.py:22
  12.4 16.3 %collective-permute-done.6.high1 = bf16[768,1024]{1,0:T(8,128)(2,1)S(1)} collective-permute-done((bf16[768,1024]{1,0:T(8,128)(2,1)}, bf16[768,1024]{1,0:T(8,128)(2,1)S(1)}, u32[]{:S(2)}, u32[]{:S(2)}) %collective-permute-start.6) | collective-permute-done | bytes 1572896 | tf_op jit(solution)/shard_map/ppermute | solution.py:22
  28.7 5.8 %collective-permute-start.7 = (bf16[768,1024]{1,0:T(8,128)(2,1)S(1)}, bf16[768,1024]{1,0:T(8,128)(2,1)S(1)}, u32[]{:S(2)}, u32[]{:S(2)}) collective-permute-start(bf16[768,1024]{1,0:T(8,128)(2,1)S(1)} %collective-permute-done.6.high1), channel_id=1, source_target_pairs={{4,0},{8,4},{12,8},{16,12},{20,16},{24,20},{28,24},{32,28},{36,32}... | collective-permute-start | bytes 4718600 | tf_op jit(solution)/shard_map/ppermute | solution.py:22
  34.5 0.0 collective-permute-done.4.low1
  34.6 1.9 %collective-permute-start.5 = (bf16[768,1024]{1,0:T(8,128)(2,1)S(1)}, bf16[768,1024]{1,0:T(8,128)(2,1)S(1)}, u32[]{:S(2)}, u32[]{:S(2)}) collective-permute-start(bf16[768,1024]{1,0:T(8,128)(2,1)S(1)} %collective-permute-done.4.low1), channel_id=1, source_target_pairs={{0,4},{4,8},{8,12},{12,16},{16,20},{20,24},{24,28},{28,32},{32,36}... | collective-permute-start | bytes 4718600 | tf_op jit(solution)/shard_map/ppermute | solution.py:22
  36.5 11.7 %collective-permute-done.1.above = bf16[4,256,1024]{2,1,0:T(8,128)(2,1)S(1)} collective-permute-done((bf16[4,256,1024]{2,1,0:T(8,128)(2,1)}, bf16[4,256,1024]{2,1,0:T(8,128)(2,1)S(1)}, u32[]{:S(2)}, u32[]{:S(2)}) %collective-permute-start.1) | collective-permute-done | bytes 2097184 | tf_op jit(solution)/shard_map/ppermute | solution.py:27
  48.2 3.3 %collective-permute-done.below = bf16[4,256,1024]{2,1,0:T(8,128)(2,1)S(1)} collective-permute-done((bf16[4,256,1024]{2,1,0:T(8,128)(2,1)}, bf16[4,256,1024]{2,1,0:T(8,128)(2,1)S(1)}, u32[]{:S(2)}, u32[]{:S(2)}) %collective-permute-start) | collective-permute-done | bytes 2097184 | tf_op jit(solution)/shard_map/ppermute | solution.py:27
  51.5 0.2 shard_map.46
  51.7 0.1 collective-permute-start.8
  51.8 3.2 %collective-permute-start.9 = (bf16[2,256,768]{2,1,0:T(8,128)(2,1)S(1)}, bf16[2,256,768]{2,1,0:T(8,128)(2,1)S(1)}, u32[]{:S(2)}, u32[]{:S(2)}) collective-permute-start(bf16[2,256,768]{2,1,0:T(8,128)(2,1)S(1)} %get-tuple-element.16), channel_id=1, source_target_pairs={{0,3},{1,0},{2,1},{3,2},{4,7},{5,4},{6,5},{7,6},{8,11},{9,8},{10,9... | collective-permute-start | bytes 2359304 | tf_op jit(solution)/shard_map/ppermute | solution.py:27
  55.0 0.0 collective-permute-start.2
  55.0 0.0 collective-permute-done.7.high2
  55.0 3.2 %collective-permute-start.3 = (bf16[2,256,256]{2,1,0:T(8,128)(2,1)S(1)}, bf16[2,256,256]{2,1,0:T(8,128)(2,1)S(1)}, u32[]{:S(2)}, u32[]{:S(2)}) collective-permute-start(bf16[2,256,256]{2,1,0:T(8,128)(2,1)S(1)} %get-tuple-element.12), channel_id=1, source_target_pairs={{0,3},{1,0},{2,1},{3,2},{4,7},{5,4},{6,5},{7,6},{8,11},{9,8},{10,9... | collective-permute-start | bytes 786440 | tf_op jit(solution)/shard_map/ppermute | solution.py:27
  58.2 0.1 collective-permute-done.5.low2
  58.4 6.7 %shard_map.47 = (f32[768,1024]{1,0:T(8,128)S(1)}, bf16[768,1024]{1,0:T(8,128)(2,1)S(1)}) custom-call(bf16[4,256,1024]{2,1,0:T(8,128)(2,1)S(1)} %collective-permute-done.below, bf16[4,256,1024]{2,1,0:T(8,128)(2,1)S(1)} %collective-permute-done.1.above, bf16[4,256,1024]{2,1,0:T(8,128)(2,1)S(1)} %bitcast.7, bf16[768,1024]{1,0:T(8,128)(2,1)S(1)} %collective-permute-done.5.low2, ...), custom_call_target="tpu_custom_call" | custom-call | flops 4294967296 | bytes 1048576 | tf_op jit(solution)/shard_map/pallas_call | solution.py:126
  65.1 8.3 %collective-permute-done.8.first = bf16[2,256,768]{2,1,0:T(8,128)(2,1)S(1)} collective-permute-done((bf16[2,256,768]{2,1,0:T(8,128)(2,1)S(1)}, bf16[2,256,768]{2,1,0:T(8,128)(2,1)S(1)}, u32[]{:S(2)}, u32[]{:S(2)}) %collective-permute-start.8) | collective-permute-done | bytes 786464 | tf_op jit(solution)/shard_map/ppermute | solution.py:27
  73.5 0.0 collective-permute-done.9.second
  73.5 2.6 %shard_map.48.rest_0_ = f32[768,1024]{1,0:T(8,128)} custom-call(bf16[2,256,768]{2,1,0:T(8,128)(2,1)S(1)} %collective-permute-done.8.first, bf16[2,256,768]{2,1,0:T(8,128)(2,1)S(1)} %collective-permute-done.9.second, f32[768,1024]{1,0:T(8,128)S(1)} %get-tuple-element.13.total, bf16[768,1024]{1,0:T(8,128)(2,1)S(1)} %get-tuple-element.14.kept), custom_call_target="tpu_custom_call" | custom-call | flops 536870912 | bytes 1048576 | tf_op jit(solution)/shard_map/pallas_call | solution.py:88
  76.1 0.6 collective-permute-done.2.first
  76.7 0.0 collective-permute-done.3.second
  76.7 1.5 %shard_map.49 = f32[768,1024]{1,0:T(8,128)} custom-call(bf16[2,256,256]{2,1,0:T(8,128)(2,1)S(1)} %collective-permute-done.2.first, bf16[2,256,256]{2,1,0:T(8,128)(2,1)S(1)} %collective-permute-done.3.second, f32[768,1024]{1,0:T(8,128)S(1)} %get-tuple-element.13.total, bf16[768,1024]{1,0:T(8,128)(2,1)S(1)} %get-tuple-element.14.kept, ...), custom_call_target="tpu_custom_call", output_to_operand_aliasing={{}: (4, {})} | custom-call | flops 536870912 | bytes 1048576 | tf_op jit(solution)/shard_map/pallas_call | solution.py:88
  (8 shorter events, 0.0 us)
Async XLA Ops:
  0.0 48.2 %collective-permute-start.1 = (bf16[4,256,1024]{2,1,0:T(8,128)(2,1)}, bf16[4,256,1024]{2,1,0:T(8,128)(2,1)S(1)}, u32[]{:S(2)}, u32[]{:S(2)}) collective-permute-start(bf16[4,256,1024]{2,1,0:T(8,128)(2,1)} %bitcast.5), channel_id=1, source_target_pairs={{0,3},{1,0},{2,1},{3,2},{4,7},{5,4},{6,5},{7,6},{8,11},{9,8},{10,9... | collective-permute-start | bytes 6291464 | tf_op jit(solution)/shard_map/ppermute | solution.py:27
  3.0 48.5 %collective-permute-start = (bf16[4,256,1024]{2,1,0:T(8,128)(2,1)}, bf16[4,256,1024]{2,1,0:T(8,128)(2,1)S(1)}, u32[]{:S(2)}, u32[]{:S(2)}) collective-permute-start(bf16[4,256,1024]{2,1,0:T(8,128)(2,1)} %bitcast.6), channel_id=1, source_target_pairs={{0,1},{1,2},{2,3},{3,0},{4,5},{5,6},{6,7},{7,4},{8,9},{9,10},{10,1... | collective-permute-start | bytes 6291464 | tf_op jit(solution)/shard_map/ppermute | solution.py:27
  3.0 55.4 %copy-start = (f32[1,768,1024]{2,1,0:T(8,128)S(1)}, f32[1,768,1024]{2,1,0:T(8,128)}, u32[]{:S(2)}) copy-start(f32[1,768,1024]{2,1,0:T(8,128)} %param.6) | copy-start | bytes 9437188
  3.0 55.4 %copy-start.1 = (bf16[1,4,256,1024]{3,2,1,0:T(8,128)(2,1)S(1)}, bf16[1,4,256,1024]{3,2,1,0:T(8,128)(2,1)}, u32[]{:S(2)}) copy-start(bf16[1,4,256,1024]{3,2,1,0:T(8,128)(2,1)} %param.5) | copy-start | bytes 6291460
  3.0 55.4 %copy-start.2 = (bf16[1,768,1024]{2,1,0:T(8,128)(2,1)S(1)}, bf16[1,768,1024]{2,1,0:T(8,128)(2,1)}, u32[]{:S(2)}) copy-start(bf16[1,768,1024]{2,1,0:T(8,128)(2,1)} %param.4) | copy-start | bytes 4718596
  3.0 55.4 %copy-start.3 = (s32[1,4]{1,0:T(1,128)S(1)}, s32[1,4]{1,0:T(1,128)}, u32[]{:S(2)}) copy-start(s32[1,4]{1,0:T(1,128)} %listed.1) | copy-start | bytes 52
  3.0 25.7 %collective-permute-start.6 = (bf16[768,1024]{1,0:T(8,128)(2,1)}, bf16[768,1024]{1,0:T(8,128)(2,1)S(1)}, u32[]{:S(2)}, u32[]{:S(2)}) collective-permute-start(bf16[768,1024]{1,0:T(8,128)(2,1)} %bitcast.8), channel_id=1, source_target_pairs={{4,0},{8,4},{12,8},{16,12},{20,16},{24,20},{28,24},{32,28},{36,32}... | collective-permute-start | bytes 4718600 | tf_op jit(solution)/shard_map/ppermute | solution.py:22
  10.5 24.1 %collective-permute-start.4 = (bf16[768,1024]{1,0:T(8,128)(2,1)}, bf16[768,1024]{1,0:T(8,128)(2,1)S(1)}, u32[]{:S(2)}, u32[]{:S(2)}) collective-permute-start(bf16[768,1024]{1,0:T(8,128)(2,1)} %bitcast.9), channel_id=1, source_target_pairs={{0,4},{4,8},{8,12},{12,16},{16,20},{20,24},{24,28},{28,32},{32,36}... | collective-permute-start | bytes 4718600 | tf_op jit(solution)/shard_map/ppermute | solution.py:22
  28.7 26.3 %collective-permute-start.7 = (bf16[768,1024]{1,0:T(8,128)(2,1)S(1)}, bf16[768,1024]{1,0:T(8,128)(2,1)S(1)}, u32[]{:S(2)}, u32[]{:S(2)}) collective-permute-start(bf16[768,1024]{1,0:T(8,128)(2,1)S(1)} %collective-permute-done.6.high1), channel_id=1, source_target_pairs={{4,0},{8,4},{12,8},{16,12},{20,16},{24,20},{28,24},{32,28},{36,32}... | collective-permute-start | bytes 4718600 | tf_op jit(solution)/shard_map/ppermute | solution.py:22
  34.6 23.8 %collective-permute-start.5 = (bf16[768,1024]{1,0:T(8,128)(2,1)S(1)}, bf16[768,1024]{1,0:T(8,128)(2,1)S(1)}, u32[]{:S(2)}, u32[]{:S(2)}) collective-permute-start(bf16[768,1024]{1,0:T(8,128)(2,1)S(1)} %collective-permute-done.4.low1), channel_id=1, source_target_pairs={{0,4},{4,8},{8,12},{12,16},{16,20},{20,24},{24,28},{28,32},{32,36}... | collective-permute-start | bytes 4718600 | tf_op jit(solution)/shard_map/ppermute | solution.py:22
  51.7 21.8 %collective-permute-start.8 = (bf16[2,256,768]{2,1,0:T(8,128)(2,1)S(1)}, bf16[2,256,768]{2,1,0:T(8,128)(2,1)S(1)}, u32[]{:S(2)}, u32[]{:S(2)}) collective-permute-start(bf16[2,256,768]{2,1,0:T(8,128)(2,1)S(1)} %get-tuple-element.15), channel_id=1, source_target_pairs={{0,1},{1,2},{2,3},{3,0},{4,5},{5,6},{6,7},{7,4},{8,9},{9,10},{10,1... | collective-permute-start | bytes 2359304 | tf_op jit(solution)/shard_map/ppermute | solution.py:27
  51.8 21.7 %collective-permute-start.9 = (bf16[2,256,768]{2,1,0:T(8,128)(2,1)S(1)}, bf16[2,256,768]{2,1,0:T(8,128)(2,1)S(1)}, u32[]{:S(2)}, u32[]{:S(2)}) collective-permute-start(bf16[2,256,768]{2,1,0:T(8,128)(2,1)S(1)} %get-tuple-element.16), channel_id=1, source_target_pairs={{0,3},{1,0},{2,1},{3,2},{4,7},{5,4},{6,5},{7,6},{8,11},{9,8},{10,9... | collective-permute-start | bytes 2359304 | tf_op jit(solution)/shard_map/ppermute | solution.py:27
  55.0 21.7 %collective-permute-start.2 = (bf16[2,256,256]{2,1,0:T(8,128)(2,1)S(1)}, bf16[2,256,256]{2,1,0:T(8,128)(2,1)S(1)}, u32[]{:S(2)}, u32[]{:S(2)}) collective-permute-start(bf16[2,256,256]{2,1,0:T(8,128)(2,1)S(1)} %get-tuple-element.11), channel_id=1, source_target_pairs={{0,1},{1,2},{2,3},{3,0},{4,5},{5,6},{6,7},{7,4},{8,9},{9,10},{10,1... | collective-permute-start | bytes 786440 | tf_op jit(solution)/shard_map/ppermute | solution.py:27
  55.0 21.7 %collective-permute-start.3 = (bf16[2,256,256]{2,1,0:T(8,128)(2,1)S(1)}, bf16[2,256,256]{2,1,0:T(8,128)(2,1)S(1)}, u32[]{:S(2)}, u32[]{:S(2)}) collective-permute-start(bf16[2,256,256]{2,1,0:T(8,128)(2,1)S(1)} %get-tuple-element.12), channel_id=1, source_target_pairs={{0,3},{1,0},{2,1},{3,2},{4,7},{5,4},{6,5},{7,6},{8,11},{9,8},{10,9... | collective-permute-start | bytes 786440 | tf_op jit(solution)/shard_map/ppermute | solution.py:27

commit v3 on v2

--- a/solution.py
+++ b/solution.py
@@ -10,6 +10,7 @@
 REACH = 2
 SLOTS = 4
 FRONT = 768
+PARTS = 3
 MIB = 1024 * 1024
 VMEM = pl.BlockSpec(memory_space=pltpu.VMEM)
 SMEM = pl.BlockSpec(memory_space=pltpu.SMEM)
@@ -58,25 +59,38 @@
         total[:, begin : begin + lanes] = value
 
 
-def split_kernel(below, above, *pieces):
+def split_kernel(begin, source, front, back):
     half = SLOTS // 2
-    for source, begin, (front, back) in ((below, 0, pieces[:2]), (above, half, pieces[2:])):
-        front[...] = source[begin : begin + half, :, :FRONT]
-        back[...] = source[begin : begin + half, :, FRONT:]
+    front[...] = source[begin : begin + half, :, :FRONT]
+    back[...] = source[begin : begin + half, :, FRONT:]
+
+
+def split(begin, source, flops):
+    half, width, columns = SLOTS // 2, source.shape[1], source.shape[2]
+    return pl.pallas_call(
+        functools.partial(split_kernel, begin),
+        out_shape=[
+            jax.ShapeDtypeStruct((half, width, FRONT), source.dtype),
+            jax.ShapeDtypeStruct((half, width, columns - FRONT), source.dtype),
+        ],
+        in_specs=[VMEM],
+        out_specs=[VMEM] * 2,
+        compiler_params=pltpu.CompilerParams(vmem_limit_bytes=4 * MIB),
+        cost_estimate=pl.CostEstimate(flops=flops, bytes_accessed=0, transcendentals=0),
+    )(source)
 
 
 def far_kernel(begin, first, second, total, kept, *rest):
     out, staged, sems = rest[-3:]
+    rows, width = staged.shape
     half = first.shape[0] * first.shape[1]
-    lanes = 256
     copies = []
-    for tile in range(first.shape[2] // lanes):
-        piece = slice(tile * lanes, (tile + 1) * lanes)
-        here = slice(begin + tile * lanes, begin + (tile + 1) * lanes)
-        value = jnp.dot(kept[:, :half], first[:, :, piece].reshape(half, lanes), preferred_element_type=jnp.float32)
-        value += jnp.dot(kept[:, half:], second[:, :, piece].reshape(half, lanes), preferred_element_type=jnp.float32)
-        staged[:, piece] = total[:, here] + value
-        copies.append(pltpu.make_async_copy(staged.at[:, piece], out.at[:, here], sems.at[tile]))
+    for tile in range(PARTS):
+        here = slice(tile * rows // PARTS, (tile + 1) * rows // PARTS)
+        value = jnp.dot(kept[here, :half], first[...].reshape(half, width), preferred_element_type=jnp.float32)
+        value += jnp.dot(kept[here, half:], second[...].reshape(half, width), preferred_element_type=jnp.float32)
+        staged[here, :] = total[here, begin : begin + width] + value
+        copies.append(pltpu.make_async_copy(staged.at[here], out.at[here, begin : begin + width], sems.at[tile]))
         copies[-1].start()
     for copy in copies:
         copy.wait()
@@ -109,19 +123,10 @@
     high1 = shifted(own, "tile", -1)
     low2 = shifted(low1, "tile", 1)
     high2 = shifted(high1, "tile", -1)
-    half = SLOTS // 2
-    front = jax.ShapeDtypeStruct((half, width, FRONT), mine.dtype)
-    back = jax.ShapeDtypeStruct((half, width, columns - FRONT), mine.dtype)
-    pieces = pl.pallas_call(
-        split_kernel,
-        out_shape=[front, back, front, back],
-        in_specs=[VMEM] * 2,
-        out_specs=[VMEM] * 4,
-        compiler_params=pltpu.CompilerParams(vmem_limit_bytes=4 * MIB),
-        cost_estimate=pl.CostEstimate(flops=20_000_000_000, bytes_accessed=0, transcendentals=0),
-    )(below, above)
-    first_front, second_front = turned(pieces[0], "pair", 1), turned(pieces[2], "pair", -1)
-    first_back, second_back = turned(pieces[1], "pair", 1), turned(pieces[3], "pair", -1)
+    second_pieces = split(SLOTS // 2, above, 20000000000)
+    first_pieces = split(0, below, 0)
+    second_front, second_back = (turned(piece, "pair", -1) for piece in second_pieces)
+    first_front, first_back = (turned(piece, "pair", 1) for piece in first_pieces)
 
     total, kept = pl.pallas_call(
         near_kernel,

time: 78.5 us -> 76.3 us (0.972)
  waiting for transfers between devices: 40.4 us -> 38.6 us
    ppermute x6, waiting for transfers between devices: 24 us -> 22.2 us  [turned(): lax.ppermute(block, axis, [(i, (i + distance) % size) for i in range(size)])]
  transfers between devices with their start and end apart: 10 -> 10, of which waited for: 6 -> 4; matrix products, arithmetic and copies ran while one was open for 0% -> 0% of each run, Pallas kernels for 12% -> 12%
where the time goes in v3:
time: 76.3 us; the launch traced here: 76 us
  waiting for transfers between devices  38.6 us (51%)
  starting transfers between devices  26.4 us (35%)
  Pallas kernels  10.7 us (14%)
    ppermute x6, waiting for transfers between devices, turned(): lax.ppermute(block, axis, [(i, (i + distance) % size) for i in range(size)])  22.2 us
    ppermute x4, starting transfers between devices, shifted(): return lax.ppermute(block, axis, route)  16.5 us
    ppermute x4, waiting for transfers between devices, shifted(): return lax.ppermute(block, axis, route)  16.4 us
    ppermute x6, starting transfers between devices, turned(): lax.ppermute(block, axis, [(i, (i + distance) % size) for i in range(size)])  9.86 us
    pallas_call x1, Pallas kernels, shards(): pl.pallas_call(near_kernel, out_shape=[jax.ShapeDtypeStruct((rows, column...  6.7 us
    pallas_call x2, Pallas kernels, far_columns(): pl.pallas_call(functools.partial(far_kernel, begin), out_shape=jax.ShapeD...  3.79 us
  transfers between devices with their start and end apart: 10, of which 4 were waited for; matrix products, arithmetic and copies ran while one was open for 0% of the time, Pallas kernels for 12%

profile of v3, /device:TPU:6, one launch (start us, length us, event | category | flops | bytes accessed | tf_op | source)
XLA Modules:
  0.0 76.0 jit_solution(1748023758189974970)
XLA Ops:
  0.0 1.6 %collective-permute-start = (bf16[4,256,1024]{2,1,0:T(8,128)(2,1)}, bf16[4,256,1024]{2,1,0:T(8,128)(2,1)S(1)}, u32[]{:S(2)}, u32[]{:S(2)}) collective-permute-start(bf16[4,256,1024]{2,1,0:T(8,128)(2,1)} %bitcast.5), channel_id=1, source_target_pairs={{0,1},{1,2},{2,3},{3,0},{4,5},{5,6},{6,7},{7,4},{8,9},{9,10},{10,1... | collective-permute-start | bytes 6291464 | tf_op jit(solution)/shard_map/ppermute | solution.py:28
  1.6 1.7 %collective-permute-start.2 = (bf16[4,256,1024]{2,1,0:T(8,128)(2,1)}, bf16[4,256,1024]{2,1,0:T(8,128)(2,1)S(1)}, u32[]{:S(2)}, u32[]{:S(2)}) collective-permute-start(bf16[4,256,1024]{2,1,0:T(8,128)(2,1)} %bitcast.6), channel_id=1, source_target_pairs={{0,3},{1,0},{2,1},{3,2},{4,7},{5,4},{6,5},{7,6},{8,11},{9,8},{10,9... | collective-permute-start | bytes 6291464 | tf_op jit(solution)/shard_map/ppermute | solution.py:28
  3.2 1.9 %collective-permute-start.4 = (bf16[768,1024]{1,0:T(8,128)(2,1)}, bf16[768,1024]{1,0:T(8,128)(2,1)S(1)}, u32[]{:S(2)}, u32[]{:S(2)}) collective-permute-start(bf16[768,1024]{1,0:T(8,128)(2,1)} %bitcast.8), channel_id=1, source_target_pairs={{0,4},{4,8},{8,12},{12,16},{16,20},{20,24},{24,28},{28,32},{32,36}... | collective-permute-start | bytes 4718600 | tf_op jit(solution)/shard_map/ppermute | solution.py:23
  5.2 7.0 %collective-permute-start.6 = (bf16[768,1024]{1,0:T(8,128)(2,1)}, bf16[768,1024]{1,0:T(8,128)(2,1)S(1)}, u32[]{:S(2)}, u32[]{:S(2)}) collective-permute-start(bf16[768,1024]{1,0:T(8,128)(2,1)} %bitcast.9), channel_id=1, source_target_pairs={{4,0},{8,4},{12,8},{16,12},{20,16},{24,20},{28,24},{32,28},{36,32}... | collective-permute-start | bytes 4718600 | tf_op jit(solution)/shard_map/ppermute | solution.py:23
  12.1 16.4 %collective-permute-done.4.low1 = bf16[768,1024]{1,0:T(8,128)(2,1)S(1)} collective-permute-done((bf16[768,1024]{1,0:T(8,128)(2,1)}, bf16[768,1024]{1,0:T(8,128)(2,1)S(1)}, u32[]{:S(2)}, u32[]{:S(2)}) %collective-permute-start.4) | collective-permute-done | bytes 1572896 | tf_op jit(solution)/shard_map/ppermute | solution.py:23
  28.5 1.9 %collective-permute-start.5 = (bf16[768,1024]{1,0:T(8,128)(2,1)S(1)}, bf16[768,1024]{1,0:T(8,128)(2,1)S(1)}, u32[]{:S(2)}, u32[]{:S(2)}) collective-permute-start(bf16[768,1024]{1,0:T(8,128)(2,1)S(1)} %collective-permute-done.4.low1), channel_id=1, source_target_pairs={{0,4},{4,8},{8,12},{12,16},{16,20},{20,24},{24,28},{28,32},{32,36}... | collective-permute-start | bytes 4718600 | tf_op jit(solution)/shard_map/ppermute | solution.py:23
  30.4 5.8 %collective-permute-start.7 = (bf16[768,1024]{1,0:T(8,128)(2,1)S(1)}, bf16[768,1024]{1,0:T(8,128)(2,1)S(1)}, u32[]{:S(2)}, u32[]{:S(2)}) collective-permute-start(bf16[768,1024]{1,0:T(8,128)(2,1)S(1)} %collective-permute-done.6.high1), channel_id=1, source_target_pairs={{4,0},{8,4},{12,8},{16,12},{20,16},{24,20},{28,24},{32,28},{36,32}... | collective-permute-start | bytes 4718600 | tf_op jit(solution)/shard_map/ppermute | solution.py:23
  36.2 12.7 %collective-permute-done.source.below = bf16[4,256,1024]{2,1,0:T(8,128)(2,1)S(1)} collective-permute-done((bf16[4,256,1024]{2,1,0:T(8,128)(2,1)}, bf16[4,256,1024]{2,1,0:T(8,128)(2,1)S(1)}, u32[]{:S(2)}, u32[]{:S(2)}) %collective-permute-start) | collective-permute-done | bytes 2097184 | tf_op jit(solution)/shard_map/ppermute | solution.py:28
  48.9 0.1 shard_map.46
  48.9 0.0 copy-start
  49.0 0.0 copy-start.1
  49.0 0.0 copy-start.2
  49.0 0.0 copy-start.3
  49.0 0.4 collective-permute-start.8
  49.4 0.1 shard_map.47
  49.5 3.0 %collective-permute-start.9 = (bf16[2,256,768]{2,1,0:T(8,128)(2,1)S(1)}, bf16[2,256,768]{2,1,0:T(8,128)(2,1)S(1)}, u32[]{:S(2)}, u32[]{:S(2)}) collective-permute-start(bf16[2,256,768]{2,1,0:T(8,128)(2,1)S(1)} %get-tuple-element.16), channel_id=1, source_target_pairs={{0,3},{1,0},{2,1},{3,2},{4,7},{5,4},{6,5},{7,6},{8,11},{9,8},{10,9... | collective-permute-start | bytes 2359304 | tf_op jit(solution)/shard_map/ppermute | solution.py:28
  52.5 0.0 collective-permute-start.1
  52.5 0.0 collective-permute-done.5.low2
  52.5 3.2 %collective-permute-start.3 = (bf16[2,256,256]{2,1,0:T(8,128)(2,1)S(1)}, bf16[2,256,256]{2,1,0:T(8,128)(2,1)S(1)}, u32[]{:S(2)}, u32[]{:S(2)}) collective-permute-start(bf16[2,256,256]{2,1,0:T(8,128)(2,1)S(1)} %get-tuple-element.12), channel_id=1, source_target_pairs={{0,3},{1,0},{2,1},{3,2},{4,7},{5,4},{6,5},{7,6},{8,11},{9,8},{10,9... | collective-permute-start | bytes 786440 | tf_op jit(solution)/shard_map/ppermute | solution.py:28
  55.7 6.7 %shard_map.48 = (f32[768,1024]{1,0:T(8,128)S(1)}, bf16[768,1024]{1,0:T(8,128)(2,1)S(1)}) custom-call(bf16[4,256,1024]{2,1,0:T(8,128)(2,1)S(1)} %collective-permute-done.source.below, bf16[4,256,1024]{2,1,0:T(8,128)(2,1)S(1)} %collective-permute-done.2.source.above, bf16[4,256,1024]{2,1,0:T(8,128)(2,1)S(1)} %bitcast.7, ...), custom_call_target="tpu_custom_call" | custom-call | flops 4294967296 | bytes 1048576 | tf_op jit(solution)/shard_map/pallas_call | solution.py:131
  62.5 8.3 %collective-permute-done.8.first = bf16[2,256,768]{2,1,0:T(8,128)(2,1)S(1)} collective-permute-done((bf16[2,256,768]{2,1,0:T(8,128)(2,1)S(1)}, bf16[2,256,768]{2,1,0:T(8,128)(2,1)S(1)}, u32[]{:S(2)}, u32[]{:S(2)}) %collective-permute-start.8) | collective-permute-done | bytes 786464 | tf_op jit(solution)/shard_map/ppermute | solution.py:28
  70.8 2.4 %shard_map.49.rest_0_ = f32[768,1024]{1,0:T(8,128)} custom-call(bf16[2,256,768]{2,1,0:T(8,128)(2,1)S(1)} %collective-permute-done.8.first, bf16[2,256,768]{2,1,0:T(8,128)(2,1)S(1)} %collective-permute-done.9.second, f32[768,1024]{1,0:T(8,128)S(1)} %get-tuple-element.13.total, bf16[768,1024]{1,0:T(8,128)(2,1)S(1)} %get-tuple-element.14.kept), custom_call_target="tpu_custom_call" | custom-call | flops 536870912 | bytes 1048576 | tf_op jit(solution)/shard_map/pallas_call | solution.py:102
  73.1 1.2 %collective-permute-done.1.first = bf16[2,256,256]{2,1,0:T(8,128)(2,1)S(1)} collective-permute-done((bf16[2,256,256]{2,1,0:T(8,128)(2,1)S(1)}, bf16[2,256,256]{2,1,0:T(8,128)(2,1)S(1)}, u32[]{:S(2)}, u32[]{:S(2)}) %collective-permute-start.1) | collective-permute-done | bytes 262176 | tf_op jit(solution)/shard_map/ppermute | solution.py:28
  74.4 1.4 %shard_map.50 = f32[768,1024]{1,0:T(8,128)} custom-call(bf16[2,256,256]{2,1,0:T(8,128)(2,1)S(1)} %collective-permute-done.1.first, bf16[2,256,256]{2,1,0:T(8,128)(2,1)S(1)} %collective-permute-done.3.second, f32[768,1024]{1,0:T(8,128)S(1)} %get-tuple-element.13.total, bf16[768,1024]{1,0:T(8,128)(2,1)S(1)} %get-tuple-element.14.kept, ...), custom_call_target="tpu_custom_call", output_to_operand_aliasing={{}: (4, {})} | custom-call | flops 536870912 | bytes 1048576 | tf_op jit(solution)/shard_map/pallas_call | solution.py:102
  (9 shorter events, 0.0 us)
Async XLA Ops:
  0.0 48.9 %collective-permute-start = (bf16[4,256,1024]{2,1,0:T(8,128)(2,1)}, bf16[4,256,1024]{2,1,0:T(8,128)(2,1)S(1)}, u32[]{:S(2)}, u32[]{:S(2)}) collective-permute-start(bf16[4,256,1024]{2,1,0:T(8,128)(2,1)} %bitcast.5), channel_id=1, source_target_pairs={{0,1},{1,2},{2,3},{3,0},{4,5},{5,6},{6,7},{7,4},{8,9},{9,10},{10,1... | collective-permute-start | bytes 6291464 | tf_op jit(solution)/shard_map/ppermute | solution.py:28
  1.6 47.8 %collective-permute-start.2 = (bf16[4,256,1024]{2,1,0:T(8,128)(2,1)}, bf16[4,256,1024]{2,1,0:T(8,128)(2,1)S(1)}, u32[]{:S(2)}, u32[]{:S(2)}) collective-permute-start(bf16[4,256,1024]{2,1,0:T(8,128)(2,1)} %bitcast.6), channel_id=1, source_target_pairs={{0,3},{1,0},{2,1},{3,2},{4,7},{5,4},{6,5},{7,6},{8,11},{9,8},{10,9... | collective-permute-start | bytes 6291464 | tf_op jit(solution)/shard_map/ppermute | solution.py:28
  3.2 25.3 %collective-permute-start.4 = (bf16[768,1024]{1,0:T(8,128)(2,1)}, bf16[768,1024]{1,0:T(8,128)(2,1)S(1)}, u32[]{:S(2)}, u32[]{:S(2)}) collective-permute-start(bf16[768,1024]{1,0:T(8,128)(2,1)} %bitcast.8), channel_id=1, source_target_pairs={{0,4},{4,8},{8,12},{12,16},{16,20},{20,24},{24,28},{28,32},{32,36}... | collective-permute-start | bytes 4718600 | tf_op jit(solution)/shard_map/ppermute | solution.py:23
  5.2 25.3 %collective-permute-start.6 = (bf16[768,1024]{1,0:T(8,128)(2,1)}, bf16[768,1024]{1,0:T(8,128)(2,1)S(1)}, u32[]{:S(2)}, u32[]{:S(2)}) collective-permute-start(bf16[768,1024]{1,0:T(8,128)(2,1)} %bitcast.9), channel_id=1, source_target_pairs={{4,0},{8,4},{12,8},{16,12},{20,16},{24,20},{28,24},{32,28},{36,32}... | collective-permute-start | bytes 4718600 | tf_op jit(solution)/shard_map/ppermute | solution.py:23
  28.5 24.0 %collective-permute-start.5 = (bf16[768,1024]{1,0:T(8,128)(2,1)S(1)}, bf16[768,1024]{1,0:T(8,128)(2,1)S(1)}, u32[]{:S(2)}, u32[]{:S(2)}) collective-permute-start(bf16[768,1024]{1,0:T(8,128)(2,1)S(1)} %collective-permute-done.4.low1), channel_id=1, source_target_pairs={{0,4},{4,8},{8,12},{12,16},{16,20},{20,24},{24,28},{28,32},{32,36}... | collective-permute-start | bytes 4718600 | tf_op jit(solution)/shard_map/ppermute | solution.py:23
  30.4 25.3 %collective-permute-start.7 = (bf16[768,1024]{1,0:T(8,128)(2,1)S(1)}, bf16[768,1024]{1,0:T(8,128)(2,1)S(1)}, u32[]{:S(2)}, u32[]{:S(2)}) collective-permute-start(bf16[768,1024]{1,0:T(8,128)(2,1)S(1)} %collective-permute-done.6.high1), channel_id=1, source_target_pairs={{4,0},{8,4},{12,8},{16,12},{20,16},{24,20},{28,24},{32,28},{36,32}... | collective-permute-start | bytes 4718600 | tf_op jit(solution)/shard_map/ppermute | solution.py:23
  48.9 6.8 %copy-start = (f32[1,768,1024]{2,1,0:T(8,128)S(1)}, f32[1,768,1024]{2,1,0:T(8,128)}, u32[]{:S(2)}) copy-start(f32[1,768,1024]{2,1,0:T(8,128)} %param.6) | copy-start | bytes 9437188
  49.0 6.8 %copy-start.1 = (bf16[1,4,256,1024]{3,2,1,0:T(8,128)(2,1)S(1)}, bf16[1,4,256,1024]{3,2,1,0:T(8,128)(2,1)}, u32[]{:S(2)}) copy-start(bf16[1,4,256,1024]{3,2,1,0:T(8,128)(2,1)} %param.5) | copy-start | bytes 6291460
  49.0 6.8 %copy-start.2 = (bf16[1,768,1024]{2,1,0:T(8,128)(2,1)S(1)}, bf16[1,768,1024]{2,1,0:T(8,128)(2,1)}, u32[]{:S(2)}) copy-start(bf16[1,768,1024]{2,1,0:T(8,128)(2,1)} %param.4) | copy-start | bytes 4718596
  49.0 6.8 %copy-start.3 = (s32[1,4]{1,0:T(1,128)S(1)}, s32[1,4]{1,0:T(1,128)}, u32[]{:S(2)}) copy-start(s32[1,4]{1,0:T(1,128)} %listed.1) | copy-start | bytes 52
  49.0 21.8 %collective-permute-start.8 = (bf16[2,256,768]{2,1,0:T(8,128)(2,1)S(1)}, bf16[2,256,768]{2,1,0:T(8,128)(2,1)S(1)}, u32[]{:S(2)}, u32[]{:S(2)}) collective-permute-start(bf16[2,256,768]{2,1,0:T(8,128)(2,1)S(1)} %get-tuple-element.15), channel_id=1, source_target_pairs={{0,1},{1,2},{2,3},{3,0},{4,5},{5,6},{6,7},{7,4},{8,9},{9,10},{10,1... | collective-permute-start | bytes 2359304 | tf_op jit(solution)/shard_map/ppermute | solution.py:28
  49.5 21.3 %collective-permute-start.9 = (bf16[2,256,768]{2,1,0:T(8,128)(2,1)S(1)}, bf16[2,256,768]{2,1,0:T(8,128)(2,1)S(1)}, u32[]{:S(2)}, u32[]{:S(2)}) collective-permute-start(bf16[2,256,768]{2,1,0:T(8,128)(2,1)S(1)} %get-tuple-element.16), channel_id=1, source_target_pairs={{0,3},{1,0},{2,1},{3,2},{4,7},{5,4},{6,5},{7,6},{8,11},{9,8},{10,9... | collective-permute-start | bytes 2359304 | tf_op jit(solution)/shard_map/ppermute | solution.py:28
  52.5 21.9 %collective-permute-start.1 = (bf16[2,256,256]{2,1,0:T(8,128)(2,1)S(1)}, bf16[2,256,256]{2,1,0:T(8,128)(2,1)S(1)}, u32[]{:S(2)}, u32[]{:S(2)}) collective-permute-start(bf16[2,256,256]{2,1,0:T(8,128)(2,1)S(1)} %get-tuple-element.11), channel_id=1, source_target_pairs={{0,1},{1,2},{2,3},{3,0},{4,5},{5,6},{6,7},{7,4},{8,9},{9,10},{10,1... | collective-permute-start | bytes 786440 | tf_op jit(solution)/shard_map/ppermute | solution.py:28
  52.5 21.9 %collective-permute-start.3 = (bf16[2,256,256]{2,1,0:T(8,128)(2,1)S(1)}, bf16[2,256,256]{2,1,0:T(8,128)(2,1)S(1)}, u32[]{:S(2)}, u32[]{:S(2)}) collective-permute-start(bf16[2,256,256]{2,1,0:T(8,128)(2,1)S(1)} %get-tuple-element.12), channel_id=1, source_target_pairs={{0,3},{1,0},{2,1},{3,2},{4,7},{5,4},{6,5},{7,6},{8,11},{9,8},{10,9... | collective-permute-start | bytes 786440 | tf_op jit(solution)/shard_map/ppermute | solution.py:28

commit v4 on v3

--- a/solution.py
+++ b/solution.py
@@ -11,6 +11,7 @@
 SLOTS = 4
 FRONT = 768
 PARTS = 3
+DIRECT = 16
 MIB = 1024 * 1024
 VMEM = pl.BlockSpec(memory_space=pltpu.VMEM)
 SMEM = pl.BlockSpec(memory_space=pltpu.SMEM)
@@ -28,7 +29,7 @@
     return lax.ppermute(block, axis, [(i, (i + distance) % size) for i in range(size)])
 
 
-def near_kernel(below, above, mine, low2, low1, own, high1, high2, residual, listed, total, kept, chosen):
+def near_kernel(straight, below, above, mine, low2, low1, own, high1, high2, residual, listed, total, kept, chosen):
     rows = residual.shape[0]
     width = mine.shape[1]
     myself = lax.axis_index("tile")
@@ -50,45 +51,81 @@
                     else:
                         kept[:, slot * width : (slot + 1) * width] = part
 
+    ends = [kept[:, (slot + 1) * width - DIRECT : (slot + 1) * width] for slot in range(SLOTS)]
+    tail = jnp.concatenate(ends, axis=1)
     lanes = 256
     for begin in range(0, residual.shape[1], lanes):
         value = residual[:, begin : begin + lanes]
         for turn, shard in enumerate((mine, below, above)):
             right = shard[:, :, begin : begin + lanes].reshape(SLOTS * width, lanes)
             value += jnp.dot(chosen[turn], right, preferred_element_type=jnp.float32)
+        value += jnp.dot(tail, straight[:, :, begin : begin + lanes].reshape(SLOTS * DIRECT, lanes), preferred_element_type=jnp.float32)
         total[:, begin : begin + lanes] = value
 
 
-def split_kernel(begin, source, front, back):
+def ends_kernel(blocks, out, sems):
+    rows = blocks.shape[1]
+    copies = []
+    for slot in range(SLOTS):
+        source = blocks.at[slot, pl.ds(rows - DIRECT, DIRECT)]
+        copies.append(pltpu.make_async_copy(source, out.at[slot], sems.at[slot]))
+        copies[-1].start()
+    for copy in copies:
+        copy.wait()
+
+
+def pass_kernel(given, out):
+    del given, out
+
+
+def passed(block, flops):
+    return pl.pallas_call(
+        pass_kernel,
+        out_shape=jax.ShapeDtypeStruct(block.shape, block.dtype),
+        in_specs=[VMEM],
+        out_specs=VMEM,
+        input_output_aliases={0: 0},
+        compiler_params=pltpu.CompilerParams(vmem_limit_bytes=MIB),
+        cost_estimate=pl.CostEstimate(flops=flops, bytes_accessed=0, transcendentals=0),
+    )(block)
+
+
+def split_kernel(begin, source, *rest):
+    front, back = rest[-2:]
     half = SLOTS // 2
-    front[...] = source[begin : begin + half, :, :FRONT]
-    back[...] = source[begin : begin + half, :, FRONT:]
-
-
-def split(begin, source, flops):
+    depth = front.shape[1]
+    front[...] = source[begin : begin + half, :depth, :FRONT]
+    back[...] = source[begin : begin + half, :depth, FRONT:]
+
+
+def split(begin, source, flops, *after):
     half, width, columns = SLOTS // 2, source.shape[1], source.shape[2]
     return pl.pallas_call(
         functools.partial(split_kernel, begin),
         out_shape=[
-            jax.ShapeDtypeStruct((half, width, FRONT), source.dtype),
-            jax.ShapeDtypeStruct((half, width, columns - FRONT), source.dtype),
+            jax.ShapeDtypeStruct((half, width - DIRECT, FRONT), source.dtype),
+            jax.ShapeDtypeStruct((half, width - DIRECT, columns - FRONT), source.dtype),
         ],
-        in_specs=[VMEM],
+        in_specs=[VMEM] + [ANY] * len(after),
         out_specs=[VMEM] * 2,
         compiler_params=pltpu.CompilerParams(vmem_limit_bytes=4 * MIB),
         cost_estimate=pl.CostEstimate(flops=flops, bytes_accessed=0, transcendentals=0),
-    )(source)
+    )(source, *after)
 
 
 def far_kernel(begin, first, second, total, kept, *rest):
     out, staged, sems = rest[-3:]
     rows, width = staged.shape
-    half = first.shape[0] * first.shape[1]
+    half, depth = first.shape[:2]
+    block = kept.shape[1] // SLOTS
     copies = []
     for tile in range(PARTS):
         here = slice(tile * rows // PARTS, (tile + 1) * rows // PARTS)
-        value = jnp.dot(kept[here, :half], first[...].reshape(half, width), preferred_element_type=jnp.float32)
-        value += jnp.dot(kept[here, half:], second[...].reshape(half, width), preferred_element_type=jnp.float32)
+        value = 0.0
+        for slot in range(SLOTS):
+            piece = (first if slot < half else second)[slot % half]
+            left = kept[here, slot * block : slot * block + depth]
+            value += jnp.dot(left, piece, preferred_element_type=jnp.float32)
         staged[here, :] = total[here, begin : begin + width] + value
         copies.append(pltpu.make_async_copy(staged.at[here], out.at[here, begin : begin + width], sems.at[tile]))
         copies[-1].start()
@@ -119,12 +156,22 @@
 
     below = turned(mine, "pair", 1)
     above = turned(mine, "pair", -1)
+    ends = pl.pallas_call(
+        ends_kernel,
+        out_shape=jax.ShapeDtypeStruct((SLOTS, DIRECT, columns), mine.dtype),
+        in_specs=[pl.BlockSpec(memory_space=pltpu.HBM)],
+        out_specs=VMEM,
+        scratch_shapes=[pltpu.SemaphoreType.DMA((SLOTS,))],
+        compiler_params=pltpu.CompilerParams(vmem_limit_bytes=MIB),
+        cost_estimate=pl.CostEstimate(flops=0, bytes_accessed=0, transcendentals=0),
+    )(pltpu.with_memory_space_constraint(mine, pltpu.HBM))
+    straight = passed(turned(ends, "pair", 2), 5000000000)
     low1 = shifted(own, "tile", 1)
     high1 = shifted(own, "tile", -1)
     low2 = shifted(low1, "tile", 1)
     high2 = shifted(high1, "tile", -1)
-    second_pieces = split(SLOTS // 2, above, 20000000000)
     first_pieces = split(0, below, 0)
+    second_pieces = split(SLOTS // 2, above, 20000000000, first_pieces[0])
     second_front, second_back = (turned(piece, "pair", -1) for piece in second_pieces)
     first_front, first_back = (turned(piece, "pair", 1) for piece in first_pieces)
 
@@ -134,12 +181,12 @@
             jax.ShapeDtypeStruct((rows, columns), jnp.float32),
             jax.ShapeDtypeStruct((rows, SLOTS * width), own.dtype),
         ],
-        in_specs=[VMEM] * 9 + [SMEM],
+        in_specs=[VMEM] * 10 + [SMEM],
         out_specs=[VMEM] * 2,
         scratch_shapes=[pltpu.VMEM((3, rows, SLOTS * width), own.dtype)],
         compiler_params=pltpu.CompilerParams(vmem_limit_bytes=16 * MIB),
         cost_estimate=pl.CostEstimate(flops=1 << 32, bytes_accessed=1 << 20, transcendentals=0),
-    )(below, above, mine, low2, low1, own, high1, high2, residual_in[0], shape_cols)
+    )(straight, below, above, mine, low2, low1, own, high1, high2, residual_in[0], shape_cols)
     out = far_columns(0, first_front, second_front, total, kept)
     out = far_columns(FRONT, first_back, second_back, total, kept, out)
     return out[None]

time: 76.3 us -> 75.8 us (level)
  waiting for transfers between devices: 38.6 us -> 33.8 us
  starting transfers between devices: 26.4 us -> 29.1 us
  Pallas kernels: 10.7 us -> 12.2 us
    ppermute x6 -> x7, waiting for transfers between devices: 22.2 us -> 18.7 us  [turned(): lax.ppermute(block, axis, [(i, (i + distance) % size) for i in range(size)])]
    ppermute x6 -> x7, starting transfers between devices: 9.86 us -> 12.5 us  [turned(): lax.ppermute(block, axis, [(i, (i + distance) % size) for i in range(size)])]
    ppermute x4, waiting for transfers between devices: 16.4 us -> 15.2 us  [shifted(): return lax.ppermute(block, axis, route)]
    pallas_call x0 -> x2, Pallas kernels: none -> 0.85 us  [the longest x1 0.84 us: shards(): pl.pallas_call(ends_kernel, out_shape=jax.ShapeDtypeStruct((SLOTS, DIRECT...]
  transfers between devices with their start and end apart: 10 -> 11, of which waited for: 4 -> 5; matrix products, arithmetic and copies ran while one was open for 0% -> 0% of each run, Pallas kernels for 12% -> 14%
where the time goes in v4:
time: 75.8 us; the launch traced here: 75.5 us
  waiting for transfers between devices  33.8 us (45%)
  starting transfers between devices  29.1 us (38%)
  Pallas kernels  12.2 us (16%)
    ppermute x7, waiting for transfers between devices, turned(): lax.ppermute(block, axis, [(i, (i + distance) % size) for i in range(size)])  18.7 us
    ppermute x4, starting transfers between devices, shifted(): return lax.ppermute(block, axis, route)  16.6 us
    ppermute x4, waiting for transfers between devices, shifted(): return lax.ppermute(block, axis, route)  15.2 us
    ppermute x7, starting transfers between devices, turned(): lax.ppermute(block, axis, [(i, (i + distance) % size) for i in range(size)])  12.5 us
    pallas_call x1, Pallas kernels, shards(): pl.pallas_call(near_kernel, out_shape=[jax.ShapeDtypeStruct((rows, column...  7.14 us
    pallas_call x2, Pallas kernels, far_columns(): pl.pallas_call(functools.partial(far_kernel, begin), out_shape=jax.ShapeD...  4.07 us
  transfers between devices with their start and end apart: 11, of which 5 were waited for; matrix products, arithmetic and copies ran while one was open for 0% of the time, Pallas kernels for 14%

profile of v4, /device:TPU:6, one launch (start us, length us, event | category | flops | bytes accessed | tf_op | source)
XLA Modules:
  0.0 75.5 jit_solution(15891027691555605135)
XLA Ops:
  0.0 1.6 %collective-permute-start = (bf16[4,256,1024]{2,1,0:T(8,128)(2,1)}, bf16[4,256,1024]{2,1,0:T(8,128)(2,1)S(1)}, u32[]{:S(2)}, u32[]{:S(2)}) collective-permute-start(bf16[4,256,1024]{2,1,0:T(8,128)(2,1)} %bitcast.4), channel_id=1, source_target_pairs={{0,1},{1,2},{2,3},{3,0},{4,5},{5,6},{6,7},{7,4},{8,9},{9,10},{10,1... | collective-permute-start | bytes 6291464 | tf_op jit(solution)/shard_map/ppermute | solution.py:29
  1.6 1.7 %collective-permute-start.2 = (bf16[4,256,1024]{2,1,0:T(8,128)(2,1)}, bf16[4,256,1024]{2,1,0:T(8,128)(2,1)S(1)}, u32[]{:S(2)}, u32[]{:S(2)}) collective-permute-start(bf16[4,256,1024]{2,1,0:T(8,128)(2,1)} %bitcast.5), channel_id=1, source_target_pairs={{0,3},{1,0},{2,1},{3,2},{4,7},{5,4},{6,5},{7,6},{8,11},{9,8},{10,9... | collective-permute-start | bytes 6291464 | tf_op jit(solution)/shard_map/ppermute | solution.py:29
  3.2 7.0 %collective-permute-start.7 = (bf16[768,1024]{1,0:T(8,128)(2,1)}, bf16[768,1024]{1,0:T(8,128)(2,1)S(1)}, u32[]{:S(2)}, u32[]{:S(2)}) collective-permute-start(bf16[768,1024]{1,0:T(8,128)(2,1)} %bitcast.9), channel_id=1, source_target_pairs={{4,0},{8,4},{12,8},{16,12},{20,16},{24,20},{28,24},{32,28},{36,32}... | collective-permute-start | bytes 4718600 | tf_op jit(solution)/shard_map/ppermute | solution.py:24
  10.2 1.9 %collective-permute-start.5 = (bf16[768,1024]{1,0:T(8,128)(2,1)}, bf16[768,1024]{1,0:T(8,128)(2,1)S(1)}, u32[]{:S(2)}, u32[]{:S(2)}) collective-permute-start(bf16[768,1024]{1,0:T(8,128)(2,1)} %bitcast.10), channel_id=1, source_target_pairs={{0,4},{4,8},{8,12},{12,16},{16,20},{20,24},{24,28},{28,32},{32,36}... | collective-permute-start | bytes 4718600 | tf_op jit(solution)/shard_map/ppermute | solution.py:24
  12.1 0.8 %shard_map.48 = bf16[4,16,1024]{2,1,0:T(8,128)(2,1)S(1)} custom-call(bf16[4,256,1024]{2,1,0:T(8,128)(2,1)} %bitcast.6), custom_call_target="tpu_custom_call" | custom-call | tf_op jit(solution)/shard_map/pallas_call | solution.py:159
  13.0 2.0 %collective-permute-start.4 = (bf16[4,16,1024]{2,1,0:T(8,128)(2,1)S(1)}, bf16[4,16,1024]{2,1,0:T(8,128)(2,1)S(1)}, u32[]{:S(2)}, u32[]{:S(2)}) collective-permute-start(bf16[4,16,1024]{2,1,0:T(8,128)(2,1)S(1)} %shard_map.48), channel_id=1, source_target_pairs={{0,2},{1,3},{2,0},{3,1},{4,6},{5,7},{6,4},{7,5},{8,10},{9,11},{10,... | collective-permute-start | bytes 393224 | tf_op jit(solution)/shard_map/ppermute | solution.py:29
  15.0 13.4 %collective-permute-done.7.high1 = bf16[768,1024]{1,0:T(8,128)(2,1)S(1)} collective-permute-done((bf16[768,1024]{1,0:T(8,128)(2,1)}, bf16[768,1024]{1,0:T(8,128)(2,1)S(1)}, u32[]{:S(2)}, u32[]{:S(2)}) %collective-permute-start.7) | collective-permute-done | bytes 1572896 | tf_op jit(solution)/shard_map/ppermute | solution.py:24
  28.4 5.8 %collective-permute-start.8 = (bf16[768,1024]{1,0:T(8,128)(2,1)S(1)}, bf16[768,1024]{1,0:T(8,128)(2,1)S(1)}, u32[]{:S(2)}, u32[]{:S(2)}) collective-permute-start(bf16[768,1024]{1,0:T(8,128)(2,1)S(1)} %collective-permute-done.7.high1), channel_id=1, source_target_pairs={{4,0},{8,4},{12,8},{16,12},{20,16},{24,20},{28,24},{32,28},{36,32}... | collective-permute-start | bytes 4718600 | tf_op jit(solution)/shard_map/ppermute | solution.py:24
  34.2 0.0 collective-permute-done.5.low1
  34.3 1.9 %collective-permute-start.6 = (bf16[768,1024]{1,0:T(8,128)(2,1)S(1)}, bf16[768,1024]{1,0:T(8,128)(2,1)S(1)}, u32[]{:S(2)}, u32[]{:S(2)}) collective-permute-start(bf16[768,1024]{1,0:T(8,128)(2,1)S(1)} %collective-permute-done.5.low1), channel_id=1, source_target_pairs={{0,4},{4,8},{8,12},{12,16},{16,20},{20,24},{24,28},{28,32},{32,36}... | collective-permute-start | bytes 4718600 | tf_op jit(solution)/shard_map/ppermute | solution.py:24
  36.2 12.7 %collective-permute-done.source.below = bf16[4,256,1024]{2,1,0:T(8,128)(2,1)S(1)} collective-permute-done((bf16[4,256,1024]{2,1,0:T(8,128)(2,1)}, bf16[4,256,1024]{2,1,0:T(8,128)(2,1)S(1)}, u32[]{:S(2)}, u32[]{:S(2)}) %collective-permute-start) | collective-permute-done | bytes 2097184 | tf_op jit(solution)/shard_map/ppermute | solution.py:29
  48.9 0.1 shard_map.46
  48.9 1.5 %collective-permute-start.9 = (bf16[2,240,768]{2,1,0:T(8,128)(2,1)S(1)}, bf16[2,240,768]{2,1,0:T(8,128)(2,1)S(1)}, u32[]{:S(2)}, u32[]{:S(2)}) collective-permute-start(bf16[2,240,768]{2,1,0:T(8,128)(2,1)S(1)} %get-tuple-element.12.rest_0_), channel_id=1, source_target_pairs={{0,1},{1,2},{2,3},{3,0},{4,5},{5,6},{6,7},{7,4},{8,9},{9,10},{10,1... | collective-permute-start | bytes 2211848 | tf_op jit(solution)/shard_map/ppermute | solution.py:29
  50.5 0.1 shard_map.47
  50.6 0.0 copy-start
  50.6 3.7 %collective-permute-start.10 = (bf16[2,240,768]{2,1,0:T(8,128)(2,1)S(1)}, bf16[2,240,768]{2,1,0:T(8,128)(2,1)S(1)}, u32[]{:S(2)}, u32[]{:S(2)}) collective-permute-start(bf16[2,240,768]{2,1,0:T(8,128)(2,1)S(1)} %get-tuple-element.16), channel_id=1, source_target_pairs={{0,3},{1,0},{2,1},{3,2},{4,7},{5,4},{6,5},{7,6},{8,11},{9,8},{10,9... | collective-permute-start | bytes 2211848 | tf_op jit(solution)/shard_map/ppermute | solution.py:29
  54.3 0.8 %collective-permute-start.3 = (bf16[2,240,256]{2,1,0:T(8,128)(2,1)S(1)}, bf16[2,240,256]{2,1,0:T(8,128)(2,1)S(1)}, u32[]{:S(2)}, u32[]{:S(2)}) collective-permute-start(bf16[2,240,256]{2,1,0:T(8,128)(2,1)S(1)} %get-tuple-element.13), channel_id=1, source_target_pairs={{0,3},{1,0},{2,1},{3,2},{4,7},{5,4},{6,5},{7,6},{8,11},{9,8},{10,9... | collective-permute-start | bytes 737288 | tf_op jit(solution)/shard_map/ppermute | solution.py:29
  55.1 1.3 %collective-permute-start.1 = (bf16[2,240,256]{2,1,0:T(8,128)(2,1)S(1)}, bf16[2,240,256]{2,1,0:T(8,128)(2,1)S(1)}, u32[]{:S(2)}, u32[]{:S(2)}) collective-permute-start(bf16[2,240,256]{2,1,0:T(8,128)(2,1)S(1)} %get-tuple-element.11), channel_id=1, source_target_pairs={{0,1},{1,2},{2,3},{3,0},{4,5},{5,6},{6,7},{7,4},{8,9},{9,10},{10,1... | collective-permute-start | bytes 737288 | tf_op jit(solution)/shard_map/ppermute | solution.py:29
  56.4 1.7 %collective-permute-done.6.low2 = bf16[768,1024]{1,0:T(8,128)(2,1)S(1)} collective-permute-done((bf16[768,1024]{1,0:T(8,128)(2,1)S(1)}, bf16[768,1024]{1,0:T(8,128)(2,1)S(1)}, u32[]{:S(2)}, u32[]{:S(2)}) %collective-permute-start.6) | collective-permute-done | bytes 1572896 | tf_op jit(solution)/shard_map/ppermute | solution.py:24
  58.1 7.1 %shard_map.50 = (f32[768,1024]{1,0:T(8,128)S(1)}, bf16[768,1024]{1,0:T(8,128)(2,1)S(1)}) custom-call(bf16[4,16,1024]{2,1,0:T(8,128)(2,1)S(1)} %shard_map.49.straight, bf16[4,256,1024]{2,1,0:T(8,128)(2,1)S(1)} %collective-permute-done.source.below, bf16[4,256,1024]{2,1,0:T(8,128)(2,1)S(1)} %collective-permute-done.2.source.above, ...), custom_call_target="tpu_custom_call" | custom-call | flops 4294967296 | bytes 1048576 | tf_op jit(solution)/shard_map/pallas_call | solution.py:178
  65.3 4.8 %collective-permute-done.10.second = bf16[2,240,768]{2,1,0:T(8,128)(2,1)S(1)} collective-permute-done((bf16[2,240,768]{2,1,0:T(8,128)(2,1)S(1)}, bf16[2,240,768]{2,1,0:T(8,128)(2,1)S(1)}, u32[]{:S(2)}, u32[]{:S(2)}) %collective-permute-start.10) | collective-permute-done | bytes 737312 | tf_op jit(solution)/shard_map/ppermute | solution.py:29
  70.1 2.6 %shard_map.51.rest_0_ = f32[768,1024]{1,0:T(8,128)} custom-call(bf16[2,240,768]{2,1,0:T(8,128)(2,1)S(1)} %collective-permute-done.9.first, bf16[2,240,768]{2,1,0:T(8,128)(2,1)S(1)} %collective-permute-done.10.second, f32[768,1024]{1,0:T(8,128)S(1)} %get-tuple-element.14.total, bf16[768,1024]{1,0:T(8,128)(2,1)S(1)} %get-tuple-element.15.kept), custom_call_target="tpu_custom_call" | custom-call | flops 536870912 | bytes 1048576 | tf_op jit(solution)/shard_map/pallas_call | solution.py:139
  72.8 1.1 %collective-permute-done.1.first = bf16[2,240,256]{2,1,0:T(8,128)(2,1)S(1)} collective-permute-done((bf16[2,240,256]{2,1,0:T(8,128)(2,1)S(1)}, bf16[2,240,256]{2,1,0:T(8,128)(2,1)S(1)}, u32[]{:S(2)}, u32[]{:S(2)}) %collective-permute-start.1) | collective-permute-done | bytes 245792 | tf_op jit(solution)/shard_map/ppermute | solution.py:29
  73.9 1.4 %shard_map.52 = f32[768,1024]{1,0:T(8,128)} custom-call(bf16[2,240,256]{2,1,0:T(8,128)(2,1)S(1)} %collective-permute-done.1.first, bf16[2,240,256]{2,1,0:T(8,128)(2,1)S(1)} %collective-permute-done.3.second, f32[768,1024]{1,0:T(8,128)S(1)} %get-tuple-element.14.total, bf16[768,1024]{1,0:T(8,128)(2,1)S(1)} %get-tuple-element.15.kept, ...), custom_call_target="tpu_custom_call", output_to_operand_aliasing={{}: (4, {})} | custom-call | flops 536870912 | bytes 1048576 | tf_op jit(solution)/shard_map/pallas_call | solution.py:139
  (13 shorter events, 0.0 us)
Async XLA Ops:
  0.0 48.9 %collective-permute-start = (bf16[4,256,1024]{2,1,0:T(8,128)(2,1)}, bf16[4,256,1024]{2,1,0:T(8,128)(2,1)S(1)}, u32[]{:S(2)}, u32[]{:S(2)}) collective-permute-start(bf16[4,256,1024]{2,1,0:T(8,128)(2,1)} %bitcast.4), channel_id=1, source_target_pairs={{0,1},{1,2},{2,3},{3,0},{4,5},{5,6},{6,7},{7,4},{8,9},{9,10},{10,1... | collective-permute-start | bytes 6291464 | tf_op jit(solution)/shard_map/ppermute | solution.py:29
  1.6 48.9 %collective-permute-start.2 = (bf16[4,256,1024]{2,1,0:T(8,128)(2,1)}, bf16[4,256,1024]{2,1,0:T(8,128)(2,1)S(1)}, u32[]{:S(2)}, u32[]{:S(2)}) collective-permute-start(bf16[4,256,1024]{2,1,0:T(8,128)(2,1)} %bitcast.5), channel_id=1, source_target_pairs={{0,3},{1,0},{2,1},{3,2},{4,7},{5,4},{6,5},{7,6},{8,11},{9,8},{10,9... | collective-permute-start | bytes 6291464 | tf_op jit(solution)/shard_map/ppermute | solution.py:29
  3.2 25.2 %collective-permute-start.7 = (bf16[768,1024]{1,0:T(8,128)(2,1)}, bf16[768,1024]{1,0:T(8,128)(2,1)S(1)}, u32[]{:S(2)}, u32[]{:S(2)}) collective-permute-start(bf16[768,1024]{1,0:T(8,128)(2,1)} %bitcast.9), channel_id=1, source_target_pairs={{4,0},{8,4},{12,8},{16,12},{20,16},{24,20},{28,24},{32,28},{36,32}... | collective-permute-start | bytes 4718600 | tf_op jit(solution)/shard_map/ppermute | solution.py:24
  10.2 24.1 %collective-permute-start.5 = (bf16[768,1024]{1,0:T(8,128)(2,1)}, bf16[768,1024]{1,0:T(8,128)(2,1)S(1)}, u32[]{:S(2)}, u32[]{:S(2)}) collective-permute-start(bf16[768,1024]{1,0:T(8,128)(2,1)} %bitcast.10), channel_id=1, source_target_pairs={{0,4},{4,8},{8,12},{12,16},{16,20},{20,24},{24,28},{28,32},{32,36}... | collective-permute-start | bytes 4718600 | tf_op jit(solution)/shard_map/ppermute | solution.py:24
  13.0 41.4 %collective-permute-start.4 = (bf16[4,16,1024]{2,1,0:T(8,128)(2,1)S(1)}, bf16[4,16,1024]{2,1,0:T(8,128)(2,1)S(1)}, u32[]{:S(2)}, u32[]{:S(2)}) collective-permute-start(bf16[4,16,1024]{2,1,0:T(8,128)(2,1)S(1)} %shard_map.48), channel_id=1, source_target_pairs={{0,2},{1,3},{2,0},{3,1},{4,6},{5,7},{6,4},{7,5},{8,10},{9,11},{10,... | collective-permute-start | bytes 393224 | tf_op jit(solution)/shard_map/ppermute | solution.py:29
  28.4 26.7 %collective-permute-start.8 = (bf16[768,1024]{1,0:T(8,128)(2,1)S(1)}, bf16[768,1024]{1,0:T(8,128)(2,1)S(1)}, u32[]{:S(2)}, u32[]{:S(2)}) collective-permute-start(bf16[768,1024]{1,0:T(8,128)(2,1)S(1)} %collective-permute-done.7.high1), channel_id=1, source_target_pairs={{4,0},{8,4},{12,8},{16,12},{20,16},{24,20},{28,24},{32,28},{36,32}... | collective-permute-start | bytes 4718600 | tf_op jit(solution)/shard_map/ppermute | solution.py:24
  34.3 23.8 %collective-permute-start.6 = (bf16[768,1024]{1,0:T(8,128)(2,1)S(1)}, bf16[768,1024]{1,0:T(8,128)(2,1)S(1)}, u32[]{:S(2)}, u32[]{:S(2)}) collective-permute-start(bf16[768,1024]{1,0:T(8,128)(2,1)S(1)} %collective-permute-done.5.low1), channel_id=1, source_target_pairs={{0,4},{4,8},{8,12},{12,16},{16,20},{20,24},{24,28},{28,32},{32,36}... | collective-permute-start | bytes 4718600 | tf_op jit(solution)/shard_map/ppermute | solution.py:24
  48.9 21.2 %collective-permute-start.9 = (bf16[2,240,768]{2,1,0:T(8,128)(2,1)S(1)}, bf16[2,240,768]{2,1,0:T(8,128)(2,1)S(1)}, u32[]{:S(2)}, u32[]{:S(2)}) collective-permute-start(bf16[2,240,768]{2,1,0:T(8,128)(2,1)S(1)} %get-tuple-element.12.rest_0_), channel_id=1, source_target_pairs={{0,1},{1,2},{2,3},{3,0},{4,5},{5,6},{6,7},{7,4},{8,9},{9,10},{10,1... | collective-permute-start | bytes 2211848 | tf_op jit(solution)/shard_map/ppermute | solution.py:29
  50.6 7.6 %copy-start = (bf16[1,4,256,1024]{3,2,1,0:T(8,128)(2,1)S(1)}, bf16[1,4,256,1024]{3,2,1,0:T(8,128)(2,1)}, u32[]{:S(2)}) copy-start(bf16[1,4,256,1024]{3,2,1,0:T(8,128)(2,1)} %param.5) | copy-start | bytes 6291460
  50.6 7.5 %copy-start.1 = (f32[1,768,1024]{2,1,0:T(8,128)S(1)}, f32[1,768,1024]{2,1,0:T(8,128)}, u32[]{:S(2)}) copy-start(f32[1,768,1024]{2,1,0:T(8,128)} %param.6) | copy-start | bytes 9437188
  50.6 7.5 %copy-start.2 = (bf16[1,768,1024]{2,1,0:T(8,128)(2,1)S(1)}, bf16[1,768,1024]{2,1,0:T(8,128)(2,1)}, u32[]{:S(2)}) copy-start(bf16[1,768,1024]{2,1,0:T(8,128)(2,1)} %param.4) | copy-start | bytes 4718596
  50.6 7.5 %copy-start.3 = (s32[1,4]{1,0:T(1,128)S(1)}, s32[1,4]{1,0:T(1,128)}, u32[]{:S(2)}) copy-start(s32[1,4]{1,0:T(1,128)} %listed.1) | copy-start | bytes 52
  50.6 19.5 %collective-permute-start.10 = (bf16[2,240,768]{2,1,0:T(8,128)(2,1)S(1)}, bf16[2,240,768]{2,1,0:T(8,128)(2,1)S(1)}, u32[]{:S(2)}, u32[]{:S(2)}) collective-permute-start(bf16[2,240,768]{2,1,0:T(8,128)(2,1)S(1)} %get-tuple-element.16), channel_id=1, source_target_pairs={{0,3},{1,0},{2,1},{3,2},{4,7},{5,4},{6,5},{7,6},{8,11},{9,8},{10,9... | collective-permute-start | bytes 2211848 | tf_op jit(solution)/shard_map/ppermute | solution.py:29
  54.3 18.4 %collective-permute-start.3 = (bf16[2,240,256]{2,1,0:T(8,128)(2,1)S(1)}, bf16[2,240,256]{2,1,0:T(8,128)(2,1)S(1)}, u32[]{:S(2)}, u32[]{:S(2)}) collective-permute-start(bf16[2,240,256]{2,1,0:T(8,128)(2,1)S(1)} %get-tuple-element.13), channel_id=1, source_target_pairs={{0,3},{1,0},{2,1},{3,2},{4,7},{5,4},{6,5},{7,6},{8,11},{9,8},{10,9... | collective-permute-start | bytes 737288 | tf_op jit(solution)/shard_map/ppermute | solution.py:29
  55.1 18.8 %collective-permute-start.1 = (bf16[2,240,256]{2,1,0:T(8,128)(2,1)S(1)}, bf16[2,240,256]{2,1,0:T(8,128)(2,1)S(1)}, u32[]{:S(2)}, u32[]{:S(2)}) collective-permute-start(bf16[2,240,256]{2,1,0:T(8,128)(2,1)S(1)} %get-tuple-element.11), channel_id=1, source_target_pairs={{0,1},{1,2},{2,3},{3,0},{4,5},{5,6},{6,7},{7,4},{8,9},{9,10},{10,1... | collective-permute-start | bytes 737288 | tf_op jit(solution)/shard_map/ppermute | solution.py:29

commit v5 on v4

--- a/solution.py
+++ b/solution.py
@@ -11,7 +11,7 @@
 SLOTS = 4
 FRONT = 768
 PARTS = 3
-DIRECT = 16
+DIRECT = 32
 MIB = 1024 * 1024
 VMEM = pl.BlockSpec(memory_space=pltpu.VMEM)
 SMEM = pl.BlockSpec(memory_space=pltpu.SMEM)
@@ -51,7 +51,7 @@
                     else:
                         kept[:, slot * width : (slot + 1) * width] = part
 
-    ends = [kept[:, (slot + 1) * width - DIRECT : (slot + 1) * width] for slot in range(SLOTS)]
+    ends = [kept[:, (slot + 1) * width - DIRECT : (slot + 1) * width] for slot in (SLOTS // 2 - 1, SLOTS - 1)]
     tail = jnp.concatenate(ends, axis=1)
     lanes = 256
     for begin in range(0, residual.shape[1], lanes):
@@ -59,16 +59,16 @@
         for turn, shard in enumerate((mine, below, above)):
             right = shard[:, :, begin : begin + lanes].reshape(SLOTS * width, lanes)
             value += jnp.dot(chosen[turn], right, preferred_element_type=jnp.float32)
-        value += jnp.dot(tail, straight[:, :, begin : begin + lanes].reshape(SLOTS * DIRECT, lanes), preferred_element_type=jnp.float32)
+        value += jnp.dot(tail, straight[:, :, begin : begin + lanes].reshape(2 * DIRECT, lanes), preferred_element_type=jnp.float32)
         total[:, begin : begin + lanes] = value
 
 
 def ends_kernel(blocks, out, sems):
     rows = blocks.shape[1]
     copies = []
-    for slot in range(SLOTS):
+    for index, slot in enumerate((SLOTS // 2 - 1, SLOTS - 1)):
         source = blocks.at[slot, pl.ds(rows - DIRECT, DIRECT)]
-        copies.append(pltpu.make_async_copy(source, out.at[slot], sems.at[slot]))
+        copies.append(pltpu.make_async_copy(source, out.at[index], sems.at[index]))
         copies[-1].start()
     for copy in copies:
         copy.wait()
@@ -93,9 +93,11 @@
 def split_kernel(begin, source, *rest):
     front, back = rest[-2:]
     half = SLOTS // 2
-    depth = front.shape[1]
-    front[...] = source[begin : begin + half, :depth, :FRONT]
-    back[...] = source[begin : begin + half, :depth, FRONT:]
+    for slot in range(half):
+        start = slot * source.shape[1]
+        depth = min(source.shape[1], front.shape[0] - start)
+        front[start : start + depth] = source[begin + slot, :depth, :FRONT]
+        back[start : start + depth] = source[begin + slot, :depth, FRONT:]
 
 
 def split(begin, source, flops, *after):
@@ -103,8 +105,8 @@
     return pl.pallas_call(
         functools.partial(split_kernel, begin),
         out_shape=[
-            jax.ShapeDtypeStruct((half, width - DIRECT, FRONT), source.dtype),
-            jax.ShapeDtypeStruct((half, width - DIRECT, columns - FRONT), source.dtype),
+            jax.ShapeDtypeStruct((half * width - DIRECT, FRONT), source.dtype),
+            jax.ShapeDtypeStruct((half * width - DIRECT, columns - FRONT), source.dtype),
         ],
         in_specs=[VMEM] + [ANY] * len(after),
         out_specs=[VMEM] * 2,
@@ -116,16 +118,12 @@
 def far_kernel(begin, first, second, total, kept, *rest):
     out, staged, sems = rest[-3:]
     rows, width = staged.shape
-    half, depth = first.shape[:2]
-    block = kept.shape[1] // SLOTS
+    depth, half = first.shape[0], kept.shape[1] // 2
     copies = []
     for tile in range(PARTS):
         here = slice(tile * rows // PARTS, (tile + 1) * rows // PARTS)
-        value = 0.0
-        for slot in range(SLOTS):
-            piece = (first if slot < half else second)[slot % half]
-            left = kept[here, slot * block : slot * block + depth]
-            value += jnp.dot(left, piece, preferred_element_type=jnp.float32)
+        value = jnp.dot(kept[here, :depth], first[...], preferred_element_type=jnp.float32)
+        value += jnp.dot(kept[here, half : half + depth], second[...], preferred_element_type=jnp.float32)
         staged[here, :] = total[here, begin : begin + width] + value
         copies.append(pltpu.make_async_copy(staged.at[here], out.at[here, begin : begin + width], sems.at[tile]))
         copies[-1].start()
@@ -135,7 +133,7 @@
 
 def far_columns(begin, first, second, total, kept, *out):
     rows = total.shape[0]
-    width = first.shape[2]
+    width = first.shape[1]
     return pl.pallas_call(
         functools.partial(far_kernel, begin),
         out_shape=jax.ShapeDtypeStruct(total.shape, total.dtype),
@@ -158,10 +156,10 @@
     above = turned(mine, "pair", -1)
     ends = pl.pallas_call(
         ends_kernel,
-        out_shape=jax.ShapeDtypeStruct((SLOTS, DIRECT, columns), mine.dtype),
+        out_shape=jax.ShapeDtypeStruct((2, DIRECT, columns), mine.dtype),
         in_specs=[pl.BlockSpec(memory_space=pltpu.HBM)],
         out_specs=VMEM,
-        scratch_shapes=[pltpu.SemaphoreType.DMA((SLOTS,))],
+        scratch_shapes=[pltpu.SemaphoreType.DMA((2,))],
         compiler_params=pltpu.CompilerParams(vmem_limit_bytes=MIB),
         cost_estimate=pl.CostEstimate(flops=0, bytes_accessed=0, transcendentals=0),
     )(pltpu.with_memory_space_constraint(mine, pltpu.HBM))

time: 75.8 us -> 75.7 us (level)
  transfers between devices with their start and end apart: 11 -> 11, of which waited for: 5 -> 6; matrix products, arithmetic and copies ran while one was open for 0% -> 0% of each run, Pallas kernels for 14% -> 14%
where the time goes in v5:
time: 75.7 us; the launch traced here: 75.5 us
  waiting for transfers between devices  34.1 us (45%)
  starting transfers between devices  29.1 us (38%)
  Pallas kernels  11.9 us (16%)
    ppermute x7, waiting for transfers between devices, turned(): lax.ppermute(block, axis, [(i, (i + distance) % size) for i in range(size)])  19 us
    ppermute x4, starting transfers between devices, shifted(): return lax.ppermute(block, axis, route)  16.6 us
    ppermute x4, waiting for transfers between devices, shifted(): return lax.ppermute(block, axis, route)  15.2 us
    ppermute x7, starting transfers between devices, turned(): lax.ppermute(block, axis, [(i, (i + distance) % size) for i in range(size)])  12.5 us
    pallas_call x1, Pallas kernels, shards(): pl.pallas_call(near_kernel, out_shape=[jax.ShapeDtypeStruct((rows, column...  7.13 us
    pallas_call x2, Pallas kernels, far_columns(): pl.pallas_call(functools.partial(far_kernel, begin), out_shape=jax.ShapeD...  3.78 us
  transfers between devices with their start and end apart: 11, of which 6 were waited for; matrix products, arithmetic and copies ran while one was open for 0% of the time, Pallas kernels for 14%

profile of v5, /device:TPU:6, one launch (start us, length us, event | category | flops | bytes accessed | tf_op | source)
XLA Modules:
  0.0 75.5 jit_solution(12775575273718468258)
XLA Ops:
  0.0 1.6 %collective-permute-start = (bf16[4,256,1024]{2,1,0:T(8,128)(2,1)}, bf16[4,256,1024]{2,1,0:T(8,128)(2,1)S(1)}, u32[]{:S(2)}, u32[]{:S(2)}) collective-permute-start(bf16[4,256,1024]{2,1,0:T(8,128)(2,1)} %bitcast.4), channel_id=1, source_target_pairs={{0,1},{1,2},{2,3},{3,0},{4,5},{5,6},{6,7},{7,4},{8,9},{9,10},{10,1... | collective-permute-start | bytes 6291464 | tf_op jit(solution)/shard_map/ppermute | solution.py:29
  1.6 1.7 %collective-permute-start.2 = (bf16[4,256,1024]{2,1,0:T(8,128)(2,1)}, bf16[4,256,1024]{2,1,0:T(8,128)(2,1)S(1)}, u32[]{:S(2)}, u32[]{:S(2)}) collective-permute-start(bf16[4,256,1024]{2,1,0:T(8,128)(2,1)} %bitcast.5), channel_id=1, source_target_pairs={{0,3},{1,0},{2,1},{3,2},{4,7},{5,4},{6,5},{7,6},{8,11},{9,8},{10,9... | collective-permute-start | bytes 6291464 | tf_op jit(solution)/shard_map/ppermute | solution.py:29
  3.2 7.0 %collective-permute-start.7 = (bf16[768,1024]{1,0:T(8,128)(2,1)}, bf16[768,1024]{1,0:T(8,128)(2,1)S(1)}, u32[]{:S(2)}, u32[]{:S(2)}) collective-permute-start(bf16[768,1024]{1,0:T(8,128)(2,1)} %bitcast.9), channel_id=1, source_target_pairs={{4,0},{8,4},{12,8},{16,12},{20,16},{24,20},{28,24},{32,28},{36,32}... | collective-permute-start | bytes 4718600 | tf_op jit(solution)/shard_map/ppermute | solution.py:24
  10.2 1.9 %collective-permute-start.5 = (bf16[768,1024]{1,0:T(8,128)(2,1)}, bf16[768,1024]{1,0:T(8,128)(2,1)S(1)}, u32[]{:S(2)}, u32[]{:S(2)}) collective-permute-start(bf16[768,1024]{1,0:T(8,128)(2,1)} %bitcast.10), channel_id=1, source_target_pairs={{0,4},{4,8},{8,12},{12,16},{16,20},{20,24},{24,28},{28,32},{32,36}... | collective-permute-start | bytes 4718600 | tf_op jit(solution)/shard_map/ppermute | solution.py:24
  12.1 0.9 %shard_map.48 = bf16[2,32,1024]{2,1,0:T(8,128)(2,1)S(1)} custom-call(bf16[4,256,1024]{2,1,0:T(8,128)(2,1)} %bitcast.6), custom_call_target="tpu_custom_call" | custom-call | tf_op jit(solution)/shard_map/pallas_call | solution.py:157
  13.0 2.0 %collective-permute-start.4 = (bf16[2,32,1024]{2,1,0:T(8,128)(2,1)S(1)}, bf16[2,32,1024]{2,1,0:T(8,128)(2,1)S(1)}, u32[]{:S(2)}, u32[]{:S(2)}) collective-permute-start(bf16[2,32,1024]{2,1,0:T(8,128)(2,1)S(1)} %shard_map.48), channel_id=1, source_target_pairs={{0,2},{1,3},{2,0},{3,1},{4,6},{5,7},{6,4},{7,5},{8,10},{9,11},{10,... | collective-permute-start | bytes 393224 | tf_op jit(solution)/shard_map/ppermute | solution.py:29
  15.0 13.4 %collective-permute-done.7.high1 = bf16[768,1024]{1,0:T(8,128)(2,1)S(1)} collective-permute-done((bf16[768,1024]{1,0:T(8,128)(2,1)}, bf16[768,1024]{1,0:T(8,128)(2,1)S(1)}, u32[]{:S(2)}, u32[]{:S(2)}) %collective-permute-start.7) | collective-permute-done | bytes 1572896 | tf_op jit(solution)/shard_map/ppermute | solution.py:24
  28.4 5.8 %collective-permute-start.8 = (bf16[768,1024]{1,0:T(8,128)(2,1)S(1)}, bf16[768,1024]{1,0:T(8,128)(2,1)S(1)}, u32[]{:S(2)}, u32[]{:S(2)}) collective-permute-start(bf16[768,1024]{1,0:T(8,128)(2,1)S(1)} %collective-permute-done.7.high1), channel_id=1, source_target_pairs={{4,0},{8,4},{12,8},{16,12},{20,16},{24,20},{28,24},{32,28},{36,32}... | collective-permute-start | bytes 4718600 | tf_op jit(solution)/shard_map/ppermute | solution.py:24
  34.2 0.0 collective-permute-done.5.low1
  34.3 1.9 %collective-permute-start.6 = (bf16[768,1024]{1,0:T(8,128)(2,1)S(1)}, bf16[768,1024]{1,0:T(8,128)(2,1)S(1)}, u32[]{:S(2)}, u32[]{:S(2)}) collective-permute-start(bf16[768,1024]{1,0:T(8,128)(2,1)S(1)} %collective-permute-done.5.low1), channel_id=1, source_target_pairs={{0,4},{4,8},{8,12},{12,16},{16,20},{20,24},{24,28},{28,32},{32,36}... | collective-permute-start | bytes 4718600 | tf_op jit(solution)/shard_map/ppermute | solution.py:24
  36.2 12.7 %collective-permute-done.source.below = bf16[4,256,1024]{2,1,0:T(8,128)(2,1)S(1)} collective-permute-done((bf16[4,256,1024]{2,1,0:T(8,128)(2,1)}, bf16[4,256,1024]{2,1,0:T(8,128)(2,1)S(1)}, u32[]{:S(2)}, u32[]{:S(2)}) %collective-permute-start) | collective-permute-done | bytes 2097184 | tf_op jit(solution)/shard_map/ppermute | solution.py:29
  48.9 0.1 shard_map.46
  48.9 1.5 %collective-permute-start.9 = (bf16[480,768]{1,0:T(8,128)(2,1)S(1)}, bf16[480,768]{1,0:T(8,128)(2,1)S(1)}, u32[]{:S(2)}, u32[]{:S(2)}) collective-permute-start(bf16[480,768]{1,0:T(8,128)(2,1)S(1)} %get-tuple-element.12.rest_0_), channel_id=1, source_target_pairs={{0,1},{1,2},{2,3},{3,0},{4,5},{5,6},{6,7},{7,4},{8,9},{9,10},{10,1... | collective-permute-start | bytes 2211848 | tf_op jit(solution)/shard_map/ppermute | solution.py:29
  50.5 0.1 shard_map.47
  50.6 3.7 %collective-permute-start.10 = (bf16[480,768]{1,0:T(8,128)(2,1)S(1)}, bf16[480,768]{1,0:T(8,128)(2,1)S(1)}, u32[]{:S(2)}, u32[]{:S(2)}) collective-permute-start(bf16[480,768]{1,0:T(8,128)(2,1)S(1)} %get-tuple-element.16), channel_id=1, source_target_pairs={{0,3},{1,0},{2,1},{3,2},{4,7},{5,4},{6,5},{7,6},{8,11},{9,8},{10,9... | collective-permute-start | bytes 2211848 | tf_op jit(solution)/shard_map/ppermute | solution.py:29
  54.3 0.8 %collective-permute-start.3 = (bf16[480,256]{1,0:T(8,128)(2,1)S(1)}, bf16[480,256]{1,0:T(8,128)(2,1)S(1)}, u32[]{:S(2)}, u32[]{:S(2)}) collective-permute-start(bf16[480,256]{1,0:T(8,128)(2,1)S(1)} %get-tuple-element.13), channel_id=1, source_target_pairs={{0,3},{1,0},{2,1},{3,2},{4,7},{5,4},{6,5},{7,6},{8,11},{9,8},{10,9... | collective-permute-start | bytes 737288 | tf_op jit(solution)/shard_map/ppermute | solution.py:29
  55.1 1.2 %collective-permute-start.1 = (bf16[480,256]{1,0:T(8,128)(2,1)S(1)}, bf16[480,256]{1,0:T(8,128)(2,1)S(1)}, u32[]{:S(2)}, u32[]{:S(2)}) collective-permute-start(bf16[480,256]{1,0:T(8,128)(2,1)S(1)} %get-tuple-element.11), channel_id=1, source_target_pairs={{0,1},{1,2},{2,3},{3,0},{4,5},{5,6},{6,7},{7,4},{8,9},{9,10},{10,1... | collective-permute-start | bytes 737288 | tf_op jit(solution)/shard_map/ppermute | solution.py:29
  56.3 1.8 %collective-permute-done.6.low2 = bf16[768,1024]{1,0:T(8,128)(2,1)S(1)} collective-permute-done((bf16[768,1024]{1,0:T(8,128)(2,1)S(1)}, bf16[768,1024]{1,0:T(8,128)(2,1)S(1)}, u32[]{:S(2)}, u32[]{:S(2)}) %collective-permute-start.6) | collective-permute-done | bytes 1572896 | tf_op jit(solution)/shard_map/ppermute | solution.py:24
  58.1 7.1 %shard_map.50 = (f32[768,1024]{1,0:T(8,128)S(1)}, bf16[768,1024]{1,0:T(8,128)(2,1)S(1)}) custom-call(bf16[2,32,1024]{2,1,0:T(8,128)(2,1)S(1)} %shard_map.49.straight, bf16[4,256,1024]{2,1,0:T(8,128)(2,1)S(1)} %collective-permute-done.source.below, bf16[4,256,1024]{2,1,0:T(8,128)(2,1)S(1)} %collective-permute-done.2.source.above, ...), custom_call_target="tpu_custom_call" | custom-call | flops 4294967296 | bytes 1048576 | tf_op jit(solution)/shard_map/pallas_call | solution.py:176
  65.3 4.9 %collective-permute-done.10.second = bf16[480,768]{1,0:T(8,128)(2,1)S(1)} collective-permute-done((bf16[480,768]{1,0:T(8,128)(2,1)S(1)}, bf16[480,768]{1,0:T(8,128)(2,1)S(1)}, u32[]{:S(2)}, u32[]{:S(2)}) %collective-permute-start.10) | collective-permute-done | bytes 737312 | tf_op jit(solution)/shard_map/ppermute | solution.py:29
  70.1 2.4 %shard_map.51.rest_0_ = f32[768,1024]{1,0:T(8,128)} custom-call(bf16[480,768]{1,0:T(8,128)(2,1)S(1)} %collective-permute-done.9.first, bf16[480,768]{1,0:T(8,128)(2,1)S(1)} %collective-permute-done.10.second, f32[768,1024]{1,0:T(8,128)S(1)} %get-tuple-element.14.total, bf16[768,1024]{1,0:T(8,128)(2,1)S(1)} %get-tuple-element.15.kept), custom_call_target="tpu_custom_call" | custom-call | flops 536870912 | bytes 1048576 | tf_op jit(solution)/shard_map/pallas_call | solution.py:137
  72.5 0.3 collective-permute-done.3.second
  72.8 1.2 %collective-permute-done.1.first = bf16[480,256]{1,0:T(8,128)(2,1)S(1)} collective-permute-done((bf16[480,256]{1,0:T(8,128)(2,1)S(1)}, bf16[480,256]{1,0:T(8,128)(2,1)S(1)}, u32[]{:S(2)}, u32[]{:S(2)}) %collective-permute-start.1) | collective-permute-done | bytes 245792 | tf_op jit(solution)/shard_map/ppermute | solution.py:29
  73.9 1.4 %shard_map.52 = f32[768,1024]{1,0:T(8,128)} custom-call(bf16[480,256]{1,0:T(8,128)(2,1)S(1)} %collective-permute-done.1.first, bf16[480,256]{1,0:T(8,128)(2,1)S(1)} %collective-permute-done.3.second, f32[768,1024]{1,0:T(8,128)S(1)} %get-tuple-element.14.total, bf16[768,1024]{1,0:T(8,128)(2,1)S(1)} %get-tuple-element.15.kept, ...), custom_call_target="tpu_custom_call", output_to_operand_aliasing={{}: (4, {})} | custom-call | flops 536870912 | bytes 1048576 | tf_op jit(solution)/shard_map/pallas_call | solution.py:137
  (13 shorter events, 0.0 us)
Async XLA Ops:
  0.0 48.9 %collective-permute-start = (bf16[4,256,1024]{2,1,0:T(8,128)(2,1)}, bf16[4,256,1024]{2,1,0:T(8,128)(2,1)S(1)}, u32[]{:S(2)}, u32[]{:S(2)}) collective-permute-start(bf16[4,256,1024]{2,1,0:T(8,128)(2,1)} %bitcast.4), channel_id=1, source_target_pairs={{0,1},{1,2},{2,3},{3,0},{4,5},{5,6},{6,7},{7,4},{8,9},{9,10},{10,1... | collective-permute-start | bytes 6291464 | tf_op jit(solution)/shard_map/ppermute | solution.py:29
  1.6 48.9 %collective-permute-start.2 = (bf16[4,256,1024]{2,1,0:T(8,128)(2,1)}, bf16[4,256,1024]{2,1,0:T(8,128)(2,1)S(1)}, u32[]{:S(2)}, u32[]{:S(2)}) collective-permute-start(bf16[4,256,1024]{2,1,0:T(8,128)(2,1)} %bitcast.5), channel_id=1, source_target_pairs={{0,3},{1,0},{2,1},{3,2},{4,7},{5,4},{6,5},{7,6},{8,11},{9,8},{10,9... | collective-permute-start | bytes 6291464 | tf_op jit(solution)/shard_map/ppermute | solution.py:29
  3.2 25.2 %collective-permute-start.7 = (bf16[768,1024]{1,0:T(8,128)(2,1)}, bf16[768,1024]{1,0:T(8,128)(2,1)S(1)}, u32[]{:S(2)}, u32[]{:S(2)}) collective-permute-start(bf16[768,1024]{1,0:T(8,128)(2,1)} %bitcast.9), channel_id=1, source_target_pairs={{4,0},{8,4},{12,8},{16,12},{20,16},{24,20},{28,24},{32,28},{36,32}... | collective-permute-start | bytes 4718600 | tf_op jit(solution)/shard_map/ppermute | solution.py:24
  10.2 24.1 %collective-permute-start.5 = (bf16[768,1024]{1,0:T(8,128)(2,1)}, bf16[768,1024]{1,0:T(8,128)(2,1)S(1)}, u32[]{:S(2)}, u32[]{:S(2)}) collective-permute-start(bf16[768,1024]{1,0:T(8,128)(2,1)} %bitcast.10), channel_id=1, source_target_pairs={{0,4},{4,8},{8,12},{12,16},{16,20},{20,24},{24,28},{28,32},{32,36}... | collective-permute-start | bytes 4718600 | tf_op jit(solution)/shard_map/ppermute | solution.py:24
  13.0 41.3 %collective-permute-start.4 = (bf16[2,32,1024]{2,1,0:T(8,128)(2,1)S(1)}, bf16[2,32,1024]{2,1,0:T(8,128)(2,1)S(1)}, u32[]{:S(2)}, u32[]{:S(2)}) collective-permute-start(bf16[2,32,1024]{2,1,0:T(8,128)(2,1)S(1)} %shard_map.48), channel_id=1, source_target_pairs={{0,2},{1,3},{2,0},{3,1},{4,6},{5,7},{6,4},{7,5},{8,10},{9,11},{10,... | collective-permute-start | bytes 393224 | tf_op jit(solution)/shard_map/ppermute | solution.py:29
  28.4 26.7 %collective-permute-start.8 = (bf16[768,1024]{1,0:T(8,128)(2,1)S(1)}, bf16[768,1024]{1,0:T(8,128)(2,1)S(1)}, u32[]{:S(2)}, u32[]{:S(2)}) collective-permute-start(bf16[768,1024]{1,0:T(8,128)(2,1)S(1)} %collective-permute-done.7.high1), channel_id=1, source_target_pairs={{4,0},{8,4},{12,8},{16,12},{20,16},{24,20},{28,24},{32,28},{36,32}... | collective-permute-start | bytes 4718600 | tf_op jit(solution)/shard_map/ppermute | solution.py:24
  34.3 23.8 %collective-permute-start.6 = (bf16[768,1024]{1,0:T(8,128)(2,1)S(1)}, bf16[768,1024]{1,0:T(8,128)(2,1)S(1)}, u32[]{:S(2)}, u32[]{:S(2)}) collective-permute-start(bf16[768,1024]{1,0:T(8,128)(2,1)S(1)} %collective-permute-done.5.low1), channel_id=1, source_target_pairs={{0,4},{4,8},{8,12},{12,16},{16,20},{20,24},{24,28},{28,32},{32,36}... | collective-permute-start | bytes 4718600 | tf_op jit(solution)/shard_map/ppermute | solution.py:24
  48.9 21.2 %collective-permute-start.9 = (bf16[480,768]{1,0:T(8,128)(2,1)S(1)}, bf16[480,768]{1,0:T(8,128)(2,1)S(1)}, u32[]{:S(2)}, u32[]{:S(2)}) collective-permute-start(bf16[480,768]{1,0:T(8,128)(2,1)S(1)} %get-tuple-element.12.rest_0_), channel_id=1, source_target_pairs={{0,1},{1,2},{2,3},{3,0},{4,5},{5,6},{6,7},{7,4},{8,9},{9,10},{10,1... | collective-permute-start | bytes 2211848 | tf_op jit(solution)/shard_map/ppermute | solution.py:29
  50.5 7.6 %copy-start = (bf16[1,4,256,1024]{3,2,1,0:T(8,128)(2,1)S(1)}, bf16[1,4,256,1024]{3,2,1,0:T(8,128)(2,1)}, u32[]{:S(2)}) copy-start(bf16[1,4,256,1024]{3,2,1,0:T(8,128)(2,1)} %param.5) | copy-start | bytes 6291460
  50.5 7.6 %copy-start.1 = (f32[1,768,1024]{2,1,0:T(8,128)S(1)}, f32[1,768,1024]{2,1,0:T(8,128)}, u32[]{:S(2)}) copy-start(f32[1,768,1024]{2,1,0:T(8,128)} %param.6) | copy-start | bytes 9437188
  50.6 7.6 %copy-start.2 = (bf16[1,768,1024]{2,1,0:T(8,128)(2,1)S(1)}, bf16[1,768,1024]{2,1,0:T(8,128)(2,1)}, u32[]{:S(2)}) copy-start(bf16[1,768,1024]{2,1,0:T(8,128)(2,1)} %param.4) | copy-start | bytes 4718596
  50.6 7.5 %copy-start.3 = (s32[1,4]{1,0:T(1,128)S(1)}, s32[1,4]{1,0:T(1,128)}, u32[]{:S(2)}) copy-start(s32[1,4]{1,0:T(1,128)} %listed.1) | copy-start | bytes 52
  50.6 19.5 %collective-permute-start.10 = (bf16[480,768]{1,0:T(8,128)(2,1)S(1)}, bf16[480,768]{1,0:T(8,128)(2,1)S(1)}, u32[]{:S(2)}, u32[]{:S(2)}) collective-permute-start(bf16[480,768]{1,0:T(8,128)(2,1)S(1)} %get-tuple-element.16), channel_id=1, source_target_pairs={{0,3},{1,0},{2,1},{3,2},{4,7},{5,4},{6,5},{7,6},{8,11},{9,8},{10,9... | collective-permute-start | bytes 2211848 | tf_op jit(solution)/shard_map/ppermute | solution.py:29
  54.3 18.4 %collective-permute-start.3 = (bf16[480,256]{1,0:T(8,128)(2,1)S(1)}, bf16[480,256]{1,0:T(8,128)(2,1)S(1)}, u32[]{:S(2)}, u32[]{:S(2)}) collective-permute-start(bf16[480,256]{1,0:T(8,128)(2,1)S(1)} %get-tuple-element.13), channel_id=1, source_target_pairs={{0,3},{1,0},{2,1},{3,2},{4,7},{5,4},{6,5},{7,6},{8,11},{9,8},{10,9... | collective-permute-start | bytes 737288 | tf_op jit(solution)/shard_map/ppermute | solution.py:29
  55.1 18.8 %collective-permute-start.1 = (bf16[480,256]{1,0:T(8,128)(2,1)S(1)}, bf16[480,256]{1,0:T(8,128)(2,1)S(1)}, u32[]{:S(2)}, u32[]{:S(2)}) collective-permute-start(bf16[480,256]{1,0:T(8,128)(2,1)S(1)} %get-tuple-element.11), channel_id=1, source_target_pairs={{0,1},{1,2},{2,3},{3,0},{4,5},{5,6},{6,7},{7,4},{8,9},{9,10},{10,1... | collective-permute-start | bytes 737288 | tf_op jit(solution)/shard_map/ppermute | solution.py:29
